TPU v7x, 512 devices: a whole 4x8x8 slice. The times are simulated.
512 devices in a mesh: row: 16 (over z, core), col: 32 (over y, x).
Axes of the slice: x: 4, y: 8, z: 8, core: 2. Of those that a mesh axis runs over, the one named last changes fastest.
Arguments:
- x_values: bfloat16 [16, 32, 64, 896], P('row', 'col'), may hold values from -0.875 to 0.875
- x_rows: int32 [16, 32, 14], P('row', 'col'), may hold values from -1 to 383, as said below
- x_cols: int32 [16, 32, 14], P('row', 'col'), may hold values from -1 to 383, as said below
- z_rows: int32 [16, 32, 36], P('row', 'col'), may hold values from -1 to 383, as said below
- z_cols: int32 [16, 32, 36], P('row', 'col'), may hold values from -1 to 383, as said below
Outputs:
- y_values: float32 [16, 32, 64, 896], P('row', 'col')
Inputs may be any that keep to these rules, and one draw needn't show every extreme that they name: Slot s of the device at (row, col) lists block (x_rows, x_cols); -1 in both marks an unused slot. A listed block row is congruent to the device's row index modulo the size of the row axis, a listed block column to its col index modulo the size of the col axis. No block is listed twice, and each block row and each block column of x holds at most 7 listed blocks. `x_cols`: pairs with x_rows as described there. Slot s of the device at (row, col) lists block (z_rows, z_cols) of the square's pattern; -1 in both marks an unused slot. A listed block row is congruent to the device's row index modulo the size of the row axis, a listed block column to its col index modulo the size of the col axis, and no block is listed twice. `z_cols`: pairs with z_rows as described there.
All inputs are finite; a program needn't handle non-finite values.
Results may differ from a plain program's by a relative error of at most 0.0027.
Values may be sent and summed in bfloat16 or wider, within the bound.
No kernel may reach another device: no remote copies, remote signals or barrier semaphores. Data moves between devices by JAX's collectives and lax.ppermute only.
A program may use at most 128 MiB of HBM per device.

v0:
```python
import jax
import jax.numpy as jnp
from jax import lax
from jax.sharding import PartitionSpec as P

NEIGH = 7


def as_blocks(values, width):
    count = values.shape[0]
    slots = values.shape[-1] // width
    shaped = values.reshape(count, width, slots, width).transpose(0, 2, 1, 3)
    return shaped.reshape(count * slots, width, width)


def partner_lists(own_rows, own_cols, column_rows, column_cols):
    entries = column_rows.shape[0]
    hits = (
        (column_cols[None, :] == own_cols[:, None])
        & (column_rows[None, :] >= 0)
        & (own_rows[:, None] >= 0)
    )
    score = jnp.where(hits, entries - jnp.arange(entries, dtype=jnp.int32)[None, :], 0)
    top_values, top_index = lax.top_k(score, NEIGH)
    return (top_index, top_values > 0)


def prepare(own_rows, own_cols, column_blocks, column_rows, column_cols):
    index, valid = partner_lists(own_rows, own_cols, column_rows, column_cols)
    picked = column_blocks[index]
    right = jnp.where(valid[:, :, None, None], picked, jnp.zeros_like(picked))
    want_rows = jnp.where(valid, own_rows[:, None], -2)
    want_cols = jnp.where(valid, column_rows[index], -2)
    return (right, want_rows, want_cols)


def pick_blocks(chosen, piece_blocks, piece_rows, piece_cols, want_rows, want_cols):
    entries = piece_rows.shape[0]
    hits = (
        (piece_rows[None, None, :] == want_rows[:, :, None])
        & (piece_cols[None, None, :] == want_cols[:, :, None])
        & (piece_rows >= 0)[None, None, :]
    )
    present = jnp.any(hits, axis=2)
    where_index = jnp.sum(
        jnp.where(hits, jnp.arange(entries, dtype=jnp.int32)[None, None, :], 0), axis=2
    )
    taken = piece_blocks[where_index]
    return jnp.where(present[:, :, None, None], taken, chosen)


def block_sums(left, right):
    summed = jnp.einsum("smik,smkj->sij", left, right, preferred_element_type=jnp.float32)
    return summed.transpose(1, 0, 2).reshape(summed.shape[1], summed.shape[0] * summed.shape[2])


def per_device(x_values, x_rows, x_cols, z_rows, z_cols):
    width = x_values.shape[2]
    column = (
        lax.all_gather(x_values, "row", axis=0, tiled=True),
        lax.all_gather(x_rows, "row", axis=0, tiled=True),
        lax.all_gather(x_cols, "row", axis=0, tiled=True),
    )
    column_blocks = as_blocks(column[0][:, 0], width)
    column_rows = column[1][:, 0].reshape(-1)
    column_cols = column[2][:, 0].reshape(-1)
    square_right, square_want_rows, square_want_cols = prepare(
        z_rows[0, 0], z_cols[0, 0], column_blocks, column_rows, column_cols
    )
    cube_right, cube_want_rows, cube_want_cols = prepare(
        x_rows[0, 0], x_cols[0, 0], column_blocks, column_rows, column_cols
    )
    square_empty = jnp.zeros_like(square_right)
    cube_empty = jnp.zeros_like(cube_right)
    row_group = (
        lax.all_gather(x_values, "col", axis=1, tiled=True),
        lax.all_gather(x_rows, "col", axis=1, tiled=True),
        lax.all_gather(x_cols, "col", axis=1, tiled=True),
    )
    square_left = pick_blocks(
        square_empty,
        as_blocks(row_group[0][0], width),
        row_group[1][0].reshape(-1),
        row_group[2][0].reshape(-1),
        square_want_rows,
        square_want_cols,
    )
    square = block_sums(square_left, square_right).astype(jnp.bfloat16)[None, None]
    square_group = (
        lax.all_gather(square, "col", axis=1, tiled=True),
        lax.all_gather(z_rows, "col", axis=1, tiled=True),
        lax.all_gather(z_cols, "col", axis=1, tiled=True),
    )
    cube_left = pick_blocks(
        cube_empty,
        as_blocks(square_group[0][0], width),
        square_group[1][0].reshape(-1),
        square_group[2][0].reshape(-1),
        cube_want_rows,
        cube_want_cols,
    )
    cube = block_sums(cube_left, cube_right)
    used = jnp.repeat((x_rows[0, 0] >= 0).astype(jnp.float32), width)
    result = (1.5 * x_values[0, 0].astype(jnp.float32) - 0.5 * cube) * used[None, :]
    return result[None, None]


def solution(mesh):
    placed = (
        P("row", "col", None, None),
        P("row", "col", None),
        P("row", "col", None),
        P("row", "col", None),
        P("row", "col", None),
    )
    return jax.shard_map(
        per_device,
        mesh=mesh,
        in_specs=placed,
        out_specs=P("row", "col", None, None),
        check_vma=False,
    )
```

profile of v0, /device:TPU:1, one launch (start us, length us, event | category | flops | bytes accessed | tf_op | source)
XLA Modules:
  0.0 344.1 jit_solution(7459818379282750300)
XLA Ops:
  6.5 0.7 all-gather.6.cloned.1.call-update
  7.3 0.7 all-gather.4.cloned.1.call-update
  8.1 24.5 %all_gather.28 = s32[16,1,14]{2,1,0:T(1,128)S(1)} all-gather(s32[1,1,14]{2,1,0:T(1,128)} %param.7), channel_id=1, replica_groups=mesh['row'=16,'col'=32] {'row'}, dimensions={0}, use_global_device_ids=true | all-gather | bytes 952 | tf_op jit(solution)/shard_map/all_gather | solution.py:62
  33.8 14.5 %all_gather.29 = s32[16,1,14]{2,1,0:T(1,128)S(1)} all-gather(s32[1,1,14]{2,1,0:T(1,128)} %param.6), channel_id=1, replica_groups=mesh['row'=16,'col'=32] {'row'}, dimensions={0}, use_global_device_ids=true | all-gather | bytes 952 | tf_op jit(solution)/shard_map/all_gather | solution.py:61
  49.1 29.4 %all_gather.31 = s32[1,32,14]{2,0,1:T(1,128)S(1)} all-gather(s32[1,1,14]{2,0,1:T(1,128)} %bitcast.79), channel_id=1, replica_groups=mesh['row'=16,'col'=32] {'col'}, dimensions={1}, use_global_device_ids=true | all-gather | bytes 1848 | tf_op jit(solution)/shard_map/all_gather | solution.py:77
  78.5 0.7 reduce.21
  79.3 28.2 %all_gather.32 = s32[1,32,14]{2,0,1:T(1,128)S(1)} all-gather(s32[1,1,14]{2,0,1:T(1,128)} %bitcast.77), channel_id=1, replica_groups=mesh['row'=16,'col'=32] {'col'}, dimensions={1}, use_global_device_ids=true | all-gather | bytes 1848 | tf_op jit(solution)/shard_map/all_gather | solution.py:78
  109.0 0.7 and_select_fusion
  109.7 2.9 top_k.27
  112.6 0.7 broadcast_select_fusion.1
  113.5 1.9 gather_fusion.1
  116.8 6.3 %reshape_squeeze.13 = bf16[16,64,14,64]{3,2,1,0:T(8,128)(2,1)} reshape(bf16[16,1,64,896]{3,2,1,0:T(8,128)(2,1)} %all-gather.6.cloned.1.call-done) | data formatting | bytes 3670016 | tf_op jit(solution)/shard_map/reshape;squeeze | solution.py:12
  123.1 5.0 %copy.35 = bf16[16,14,64,64]{3,2,1,0:T(8,128)(2,1)} copy(bf16[16,14,64,64]{3,1,2,0:T(8,128)(2,1)} %bitcast.70) | data formatting | bytes 3670016 | tf_op jit(solution)/shard_map/transpose | solution.py:12
  128.1 5.2 %gather_fusion.3 = bf16[252,64,64]{2,1,0:T(8,128)(2,1)} fusion(bf16[224,64,64]{2,1,0:T(8,128)(2,1)} %bitcast.66, s32[1024]{0:T(1024)S(1)} %pad_clamp_fusion.2), kind=kCustom, calls=%fused_computation.3 | custom fusion | bytes 4129776 | tf_op jit(solution)/shard_map/gather | solution.py:30
  133.3 8.7 %all-gather.4.cloned.1.call-done = bf16[1,32,64,896]{3,2,0,1:T(8,128)(2,1)} async-done(((bf16[1,1,64,896]{3,2,0,1:T(8,128)(2,1)}), bf16[1,32,64,896]{3,2,0,1:T(8,128)(2,1)}) %all-gather.4.cloned.1.call-update) | async-done | bytes 3670032 | tf_op jit(solution)/shard_map/all_gather | solution.py:76
  141.9 11.5 %reshape_squeeze.12 = bf16[32,64,14,64]{3,2,1,0:T(8,128)(2,1)} reshape(bf16[1,32,64,896]{3,2,0,1:T(8,128)(2,1)} %all-gather.4.cloned.1.call-done) | data formatting | bytes 7340032 | tf_op jit(solution)/shard_map/reshape;squeeze | solution.py:12
  153.4 8.3 %copy.33 = bf16[32,14,64,64]{3,2,1,0:T(8,128)(2,1)} copy(bf16[32,14,64,64]{3,1,2,0:T(8,128)(2,1)} %bitcast.65) | data formatting | bytes 7340032 | tf_op jit(solution)/shard_map/transpose | solution.py:12
  161.7 6.1 %gather_fusion.2 = bf16[252,64,64]{2,1,0:T(8,128)(2,1)} fusion(bf16[448,64,64]{2,1,0:T(8,128)(2,1)} %bitcast.69, s32[1024]{0:T(1024)S(1)} %pad_clamp_fusion.1), kind=kCustom, calls=%fused_computation.2 | custom fusion | bytes 4129776 | tf_op jit(solution)/shard_map/gather | solution.py:48
  167.8 5.1 %fusion.21 = bf16[64,36,64]{2,0,1:T(8,128)(2,1)S(1)} fusion(bf16[36,7,64,64]{3,2,1,0:T(8,128)(2,1)} %bitcast.71, pred[36,7]{1,0:T(8,128)(4,1)S(1)} %get-tuple-element.20, bf16[36,7,64,64]{3,2,1,0:T(8,128)(2,1)} %bitcast.72, pred[36,7]{1,0:T(8,128)(4,1)S(1)} %copy.31), kind=kOutput, calls=%fused_computation.19 | convolution fusion | flops 134332416 | bytes 4424184 | tf_op jit(solution)/shard_map/smik,smkj->sij/dot_general | solution.py:53
  173.3 1.1 convert_element_type.26
  174.6 26.7 %all_gather.27 = s32[1,32,36]{2,0,1:T(1,128)S(1)} all-gather(s32[1,1,36]{2,0,1:T(1,128)S(1)} %bitcast.82), channel_id=1, replica_groups=mesh['row'=16,'col'=32] {'col'}, dimensions={1}, use_global_device_ids=true | all-gather | bytes 4752 | tf_op jit(solution)/shard_map/all_gather | solution.py:91
  201.3 0.7 reduce.23
  202.1 28.2 %all_gather.30 = s32[1,32,36]{2,0,1:T(1,128)S(1)} all-gather(s32[1,1,36]{2,0,1:T(1,128)S(1)} %bitcast.84), channel_id=1, replica_groups=mesh['row'=16,'col'=32] {'col'}, dimensions={1}, use_global_device_ids=true | all-gather | bytes 4752 | tf_op jit(solution)/shard_map/all_gather | solution.py:92
  231.2 2.8 top_k.23
  234.2 1.3 gather_fusion
  236.8 2.9 gather_fusion.5
  239.7 44.7 %all-gather.8.cloned.1.call-done = bf16[1,32,64,2304]{3,2,0,1:T(8,128)(2,1)} async-done(((bf16[1,1,64,2304]{3,2,0,1:T(8,128)(2,1)}), bf16[1,32,64,2304]{3,2,0,1:T(8,128)(2,1)}) %all-gather.8.cloned.1.call-update) | async-done | bytes 9437200 | tf_op jit(solution)/shard_map/all_gather | solution.py:90
  284.3 27.0 %reshape_squeeze.14 = bf16[32,64,36,64]{3,2,1,0:T(8,128)(2,1)} reshape(bf16[1,32,64,2304]{3,2,0,1:T(8,128)(2,1)} %all-gather.8.cloned.1.call-done) | data formatting | bytes 18874368 | tf_op jit(solution)/shard_map/reshape;squeeze | solution.py:12
  311.4 16.8 %copy.38 = bf16[32,36,64,64]{3,2,1,0:T(8,128)(2,1)} copy(bf16[32,36,64,64]{3,1,2,0:T(8,128)(2,1)} %bitcast.64) | data formatting | bytes 18874368 | tf_op jit(solution)/shard_map/transpose | solution.py:12
  328.1 7.2 %gather_fusion.4 = bf16[98,64,64]{2,1,0:T(8,128)(2,1)S(1)} fusion(bf16[1152,64,64]{2,1,0:T(8,128)(2,1)} %bitcast.68, s32[1024]{0:T(1024)S(1)} %pad_clamp_fusion), kind=kCustom, calls=%fused_computation.4 | custom fusion | bytes 1606024 | tf_op jit(solution)/shard_map/gather | solution.py:48
  335.4 1.0 fusion.36
  336.9 0.7 subtract_multiply_fusion
  (67 shorter events, 8.5 us)
Async XLA Ops:
  6.5 110.3 %all-gather.6.cloned.1.call-start = ((), (), s32[]{:S(2)}) async-start(), calls=%async_computation.1 | async-start | bytes 1949696 | tf_op jit(solution)/shard_map/all_gather | solution.py:60
  7.3 134.7 %all-gather.4.cloned.1.call-start = ((), (), s32[]{:S(2)}) async-start(), calls=%async_computation | async-start | bytes 3784704 | tf_op jit(solution)/shard_map/all_gather | solution.py:76
  8.0 276.3 %all-gather.8.cloned.1.call-start = ((), (), s32[]{:S(2)}) async-start(), calls=%async_computation.2 | async-start | bytes 9732096 | tf_op jit(solution)/shard_map/all_gather | solution.py:90
  167.8 6.7 %copy-start.2 = (s32[1,1,14]{2,1,0:T(1,128)S(1)}, s32[1,1,14]{2,1,0:T(1,128)}, u32[]{:S(2)}) copy-start(s32[1,1,14]{2,1,0:T(1,128)} %param.6) | copy-start | bytes 172
  167.8 6.8 %copy-start.3 = (s32[1,1,36]{2,1,0:T(1,128)S(1)}, s32[1,1,36]{2,1,0:T(1,128)}, u32[]{:S(2)}) copy-start(s32[1,1,36]{2,1,0:T(1,128)} %param.8) | copy-start | bytes 436
  167.8 34.3 %copy-start.4 = (s32[1,1,36]{2,1,0:T(1,128)S(1)}, s32[1,1,36]{2,1,0:T(1,128)}, u32[]{:S(2)}) copy-start(s32[1,1,36]{2,1,0:T(1,128)} %param.9) | copy-start | bytes 436
  167.8 63.4 %copy-start.1 = (s32[1,1,14]{2,1,0:T(1,128)S(1)}, s32[1,1,14]{2,1,0:T(1,128)}, u32[]{:S(2)}) copy-start(s32[1,1,14]{2,1,0:T(1,128)} %param.7) | copy-start | bytes 172
  335.4 1.5 copy-start
Sparse Core Ops, SparseCore 0:
  9.5 48.7 all-gather.5
  61.5 80.4 all-gather.3
  174.6 109.7 all-gather.7
where the time goes:
time: 346 us; the launch traced here: 344 us
  blocking collectives  152 us (44%)
  local copies, waits for them, and re-layouts  104 us (30%)
  waiting for transfers between devices  54.8 us (16%)
  other arithmetic  14.4 us (4%)
  between operations  13.4 us (4%)
  matrix products  6.17 us (2%)
    another operation x3, local copies, waits for them, and re-layouts, as_blocks(): shaped = values.reshape(count, width, slots, width).transpose(0, 2, 1, 3)  44.8 us
    all_gather x1, waiting for transfers between devices, per_device(): lax.all_gather(square, 'col', axis=1, tiled=True)  44.7 us
    transpose x3, local copies, waits for them, and re-layouts, as_blocks(): shaped = values.reshape(count, width, slots, width).transpose(0, 2, 1, 3)  30 us
    all_gather x1, blocking collectives, per_device(): lax.all_gather(x_rows, 'col', axis=1, tiled=True)  29.4 us
    all_gather x1, blocking collectives, per_device(): lax.all_gather(z_cols, 'col', axis=1, tiled=True)  28.2 us
    all_gather x1, blocking collectives, per_device(): lax.all_gather(x_cols, 'col', axis=1, tiled=True)  28.2 us
    all_gather x1, blocking collectives, per_device(): lax.all_gather(z_rows, 'col', axis=1, tiled=True)  26.7 us
    all_gather x1, blocking collectives, per_device(): lax.all_gather(x_cols, 'row', axis=0, tiled=True)  24.5 us
  transfers between devices with their start and end apart: 3, of which 2 were waited for; matrix products, arithmetic and copies ran while one was open for 11% of the time, Pallas kernels for 0%

commit v1 on v0

v1 whole, which is shorter than its diff:
```python
import functools

import jax
import jax.numpy as jnp
from jax import lax
from jax.experimental import pallas as pl
from jax.experimental.pallas import tpu as pltpu
from jax.sharding import PartitionSpec as P

NEIGH = 7
CORES = 2
NEAR = 4
XROWS = 16
ZROWS = 40
ZSTEP = 64
SEGMENT = NEAR * ZSTEP
FIRST = 12
MORE = 2
META = 16
CODE = 512
LANES = 128
CHUNK = 2
GROUP = 8
STEP = 2
COUNT = 32
FAR = 1e9
PARAMS = pltpu.CompilerParams(vmem_limit_bytes=20 * 1024 * 1024)
VMEM = pl.BlockSpec(memory_space=pltpu.VMEM)
SMEM = pl.BlockSpec(memory_space=pltpu.SMEM)


def lane_numbers(width):
    return lax.broadcasted_iota(jnp.int32, (1, width), 1).astype(jnp.float32)


def following(hits, lanes, last):
    return jnp.min(jnp.where(hits & (lanes > last), lanes, FAR), axis=1, keepdims=True)


def picked(hits, values):
    return jnp.sum(jnp.where(hits, values, 0.0), axis=1, keepdims=True)


def put(table, base, count, good, value):
    return jnp.where((lane_numbers(LANES) == base + count) & good, value, table)


def match_kernel(own_z, own_x, row_x, row_z, col_x, square_list, cube_list):
    row_i, row_m = row_x[0:1, :], row_x[1:2, :]
    col_m, col_k = col_x[0:1, :], col_x[1:2, :]
    row_lanes, col_lanes = lane_numbers(row_i.shape[1]), lane_numbers(col_m.shape[1])
    lane = lane_numbers(LANES)

    i, k = own_z[0][:, :1], own_z[1][:, :1]
    in_row, in_col = (row_i == i) & (i >= 0), (col_k == k) & (k >= 0)
    table = jnp.zeros((ZROWS, LANES), jnp.float32)
    count = jnp.zeros((ZROWS, 1), jnp.float32)
    last = count - 1
    for _ in range(NEIGH):
        last = following(in_row, row_lanes, last)
        middle = picked(row_lanes == last, row_m)
        found = picked(in_col & (col_m == middle), col_lanes + 1)
        good = (last < FAR) & (found > 0)
        table = put(table, 0, count, good, last)
        table = put(table, 8, count, good, found - 1)
        count = count + jnp.where(good, 1.0, 0.0)
    square_list[...] = jnp.where(lane == COUNT, count, table).astype(jnp.int32)

    z_lanes = lane_numbers(row_z.shape[1])
    z_i, z_k = row_z[0:1, :], row_z[1:2, :]
    i, j = own_x[0][:, :1], own_x[1][:, :1]
    in_col = (col_k == j) & (j >= 0)
    needed = jnp.zeros((1, row_z.shape[1]), jnp.float32)
    entries = []
    last = jnp.full((XROWS, 1), -1.0, jnp.float32)
    for _ in range(NEIGH):
        last = following(in_col, col_lanes, last)
        middle = picked(col_lanes == last, col_m)
        hits = (z_i == i) & (z_k == middle) & (last < FAR)
        needed = jnp.maximum(
            needed, jnp.max(jnp.where(hits, 1.0, 0.0), axis=0, keepdims=True)
        )
        entries.append((last, picked(hits, z_lanes + 1) - 1))
    needed = jnp.concatenate(
        [needed[:, n : n + SEGMENT] for n in range(0, needed.shape[1], SEGMENT)], axis=0
    )
    before = (
        lax.broadcasted_iota(jnp.int32, (SEGMENT, SEGMENT), 0)
        < lax.broadcasted_iota(jnp.int32, (SEGMENT, SEGMENT), 1)
    ).astype(jnp.float32)
    rank = jnp.dot(needed, before, preferred_element_type=jnp.float32)
    rank = jnp.concatenate([rank[n : n + 1] for n in range(rank.shape[0])], axis=1)
    table = jnp.zeros((XROWS, LANES), jnp.float32)
    count = jnp.zeros((XROWS, 1), jnp.float32)
    for last, entry in entries:
        good = entry >= 0
        place = picked(z_lanes == entry, rank)
        group = jnp.floor(entry / SEGMENT)
        value = (group * SEGMENT + place) * SEGMENT + entry - group * SEGMENT
        table = put(table, 0, count, good, value)
        table = put(table, 8, count, good, last)
        count = count + jnp.where(good, 1.0, 0.0)
    cube_list[...] = jnp.where(lane == COUNT, count, table).astype(jnp.int32)


def send_kernel(near_z, row_x, cross_x, send_list, loads):
    row_i, row_m = row_x[0:1, :], row_x[1:2, :]
    row_lanes, lane = lane_numbers(row_i.shape[1]), lane_numbers(LANES)
    needs, numbers = [], []
    for n in range(NEAR):
        here = slice(n * ZROWS, (n + 1) * ZROWS)
        i, k = near_z[0][here, :1], near_z[1][here, :1]
        cross_k, cross_j, cross_y = (cross_x[n][t : t + 1, :] for t in range(3))
        in_row, in_cross = (row_i == i) & (i >= 0), (cross_k == k) & (k >= 0)
        need = jnp.zeros((ZROWS, LANES), jnp.float32)
        last = jnp.full((ZROWS, 1), -1.0, jnp.float32)
        for _ in range(NEIGH):
            last = following(in_cross, row_lanes, last)
            target = picked(row_lanes == last, cross_j)
            far = picked(row_lanes == last, cross_y)
            found = picked(in_row & (row_m == target), 1.0)
            need = jnp.where((lane == far) & (last < FAR) & (found > 0), 1.0, need)
        needs.append(need)
        numbers.append(lax.broadcasted_iota(jnp.int32, need.shape, 0) + n * ZSTEP)
    need = jnp.concatenate(needs, axis=0)
    number = jnp.concatenate(numbers, axis=0).astype(jnp.float32)
    size = need.shape[0]
    before = (
        lax.broadcasted_iota(jnp.int32, (size, size), 1)
        < lax.broadcasted_iota(jnp.int32, (size, size), 0)
    ).astype(jnp.float32)
    rank = jnp.dot(before, need, preferred_element_type=jnp.float32)
    rank = jnp.where(need > 0, rank, -1.0)

    def list_rank(p, carry):
        at = rank == p.astype(jnp.float32)
        row = jnp.sum(jnp.where(at, number, 0.0), axis=0, keepdims=True)
        send_list[pl.ds(p, 1), :] = row.astype(jnp.int32)
        return carry

    lax.fori_loop(0, size, list_rank, 0)
    loads[...] = jnp.sum(need, axis=0, keepdims=True).astype(jnp.int32)


def half_mask(half, good):
    lane = lax.broadcasted_iota(jnp.int32, (1, LANES), 1)
    return jnp.where((lane >> 6 == half) & (good > 0), 1.0, 0.0).astype(jnp.bfloat16)


def flat(value):
    return jnp.full((1, LANES), value.astype(jnp.float32)).astype(jnp.bfloat16)


def to_half(tile, half, want):
    swapped = jnp.concatenate([tile[:, 64:], tile[:, :64]], axis=1)
    other = (half != want).astype(jnp.int32)
    return tile * flat(1 - other) + swapped * flat(other)


def pair_up(even, odd):
    even, odd = (tile + pltpu.roll(tile, 64, 1) for tile in (even, odd))
    lane = lax.broadcasted_iota(jnp.int32, even.shape, 1)
    return jnp.where(lane < 64, even, odd)


def add_products(lists, rows, load_left, load_right, sums, chunks):
    sums[...] = jnp.zeros_like(sums)

    def per_row(n, length):
        def one(t, length):
            chunks[length] = (n << 3) + t * CHUNK
            return length + 1

        return lax.fori_loop(0, lax.div(lists[n, COUNT] + CHUNK - 1, CHUNK), one, length)

    length = lax.fori_loop(0, rows - 1, per_row, 0)
    for spare in range(GROUP):
        chunks[length + spare] = (rows - 1) << 3

    def per_group(group, carry):
        values = []
        for n in range(GROUP):
            code = chunks[group * GROUP + n]
            row, start = code >> 3, code & 7
            left, right = [], []
            for t in range(CHUNK):
                place = jnp.minimum(start + t, NEIGH - 1)
                good = (start + t < lists[row, COUNT]).astype(jnp.int32)
                left.append(load_left(lists[row, place], good))
                tile = load_right(lists[row, 8 + place])
                right += [tile, tile]
            left, right = jnp.concatenate(left, axis=1), jnp.concatenate(right, axis=0)
            values.append((row, jnp.dot(left, right, preferred_element_type=jnp.float32)))
        for row, value in values:
            sums[row] += value
        return carry

    lax.fori_loop(0, lax.div(length + GROUP - 1, GROUP), per_group, 0)


def tile_of(entry, step):
    shift = step.bit_length() - 1
    return entry >> shift, (entry & (step - 1)) >> 1, entry & 1


def rows_of(ref, tile):
    return ref.at[pl.ds(pl.multiple_of(tile * 64, 64), 64), :]


def x_tile(ref, entry):
    device, tile, half = tile_of(entry, XROWS)
    return rows_of(ref.at[device], tile)[...] * half_mask(half, 1)


def square_kernel(lists, row_tiles, col_tiles, out_ref, sums, chunks):
    def load_left(entry, good):
        device, tile, half = tile_of(entry, XROWS)
        return row_tiles[device, tile] * half_mask(half, good)

    add_products(
        lists, ZROWS, load_left, functools.partial(x_tile, col_tiles), sums, chunks
    )

    def store(n, carry):
        square = pair_up(sums[2 * n], sums[2 * n + 1]).astype(jnp.bfloat16)
        for copy in range(out_ref.shape[0]):
            out_ref[copy, n] = square
        return carry

    lax.fori_loop(0, out_ref.shape[1], store, 0, unroll=2)


def pack_kernel(info, loads, lists, near, out_ref):
    out_ref[...] = jnp.zeros_like(out_ref)
    first, own = info[0], info[1]
    places = (out_ref.shape[1] - META) // 32
    most = jnp.int32(0)
    for target in range(out_ref.shape[0]):
        most = jnp.maximum(most, jnp.where(own == target, 0, loads[0, target]))

    def per_target(target, carry):
        out_ref[target, places * 32 :, :] = jnp.broadcast_to(flat(most), (META, LANES))
        number = jnp.where(target == own, 0, loads[0, target]) - first
        number = jnp.clip(number, 0, places)

        def per_step(step, carry):
            packed = []
            for n in range(STEP):
                both = []
                for half in range(2):
                    place = step * (2 * STEP) + 2 * n + half
                    good = (place < number).astype(jnp.int32)
                    entry = lists[jnp.minimum(first + place, lists.shape[0] - 1), target]
                    device, tile, side = tile_of(entry, ZSTEP)
                    both.append(to_half(near[device, tile], side, half) * half_mask(half, good))
                packed.append(both[0] + both[1])
            for n, tile in enumerate(packed):
                rows_of(out_ref.at[target], step * STEP + n)[...] = tile
            return carry

        return lax.fori_loop(0, lax.div(number + 2 * STEP - 1, 2 * STEP), per_step, carry)

    lax.fori_loop(0, out_ref.shape[0], per_target, 0)


def cube_kernel(info, lists, near, far, col_tiles, base, out_ref, most_ref, sums, chunks):
    first, own = info[0], info[1]
    places = (far.shape[1] - META) // 32
    most = far[0, places * 32 :, :]
    for n in range(1, far.shape[0]):
        most = jnp.maximum(most, far[n, places * 32 :, :])
    most_ref[0] = jnp.max(most.astype(jnp.float32)).astype(jnp.int32)

    def load_left(code, good):
        group, rank, entry = code >> 16, (code >> 8) & 255, code & 255
        here = group == own
        close = good * (here & (first == 0)).astype(jnp.int32)
        place = rank - first
        inside = (place >= 0) & (place < places) & ~here
        away = good * inside.astype(jnp.int32)
        place = jnp.clip(place, 0, places - 1)
        device, tile, half = tile_of(entry, ZSTEP)
        left = near[device, tile] * half_mask(half, close)
        return left + rows_of(far.at[group], place >> 1)[...] * half_mask(place & 1, away)

    add_products(
        lists, XROWS, load_left, functools.partial(x_tile, col_tiles), sums, chunks
    )
    for n in range(out_ref.shape[1] // LANES):
        here = slice(n * LANES, (n + 1) * LANES)
        out_ref[:, here] = base[:, here] - 0.5 * pair_up(sums[2 * n], sums[2 * n + 1])


def call(kernel, scalars, arrays, out, scratch=()):
    single = isinstance(out, jax.ShapeDtypeStruct)
    return pl.pallas_call(
        kernel,
        out_shape=out,
        in_specs=[SMEM] * len(scalars) + [VMEM] * len(arrays),
        out_specs=VMEM if single else [SMEM if o.shape == (1,) else VMEM for o in out],
        scratch_shapes=scratch,
        compiler_params=PARAMS,
    )(*scalars, *arrays)


def sums_scratch(rows):
    return [
        pltpu.VMEM((rows, 64, LANES), jnp.float32),
        pltpu.SMEM((rows * 4 + 2 * GROUP,), jnp.int32),
    ]


def decode(codes):
    rows = jnp.where(codes >= 0, codes // CODE, -1)
    cols = jnp.where(codes >= 0, codes % CODE, -1)
    return jnp.stack([rows, cols]).astype(jnp.float32)


def encode(rows, cols, length):
    codes = jnp.where(rows >= 0, rows * CODE + cols, -1)
    return jnp.pad(codes, (0, length - codes.shape[0]), constant_values=-1)


def sublanes(pairs):
    return jnp.broadcast_to(pairs[:, :, None], (*pairs.shape, LANES))


def send_all(array, axis, count, **groups):
    copies = jnp.broadcast_to(array, (count, *array.shape))
    return lax.all_to_all(copies, axis, split_axis=0, concat_axis=0, **groups)


def per_device(x_values, x_rows, x_cols, z_rows, z_cols):
    x_rows, x_cols, z_rows, z_cols = (a[0, 0] for a in (x_rows, x_cols, z_rows, z_cols))
    own = x_values[0, 0]
    size, width = own.shape
    n_row, n_col = lax.axis_size("row"), lax.axis_size("col")
    n_far = n_col // NEAR
    col = lax.axis_index("col")
    far_own, near_own = col // NEAR, col % NEAR
    near_groups = [[y * NEAR + x for x in range(NEAR)] for y in range(n_far)]
    far_groups = [[y * NEAR + x for y in range(n_far)] for x in range(NEAR)]
    core_groups = [[z + core for z in range(0, n_row, CORES)] for core in range(CORES)]

    tiles = own.reshape(size, width // LANES, LANES).transpose(1, 0, 2)
    near_tiles = send_all(tiles, "col", NEAR, axis_index_groups=near_groups)
    row_tiles = lax.all_gather(near_tiles, "col", axis=0, axis_index_groups=far_groups)
    row_tiles = row_tiles.reshape(n_col, *tiles.shape)

    x_codes, z_codes = encode(x_rows, x_cols, XROWS), encode(z_rows, z_cols, ZROWS)
    codes = jnp.concatenate([x_codes, z_codes])
    codes = jnp.pad(codes, (0, LANES - codes.shape[0]), constant_values=-1)
    codes, near_tiles = lax.optimization_barrier((codes, near_tiles))
    codes = send_all(codes[None], "col", n_col)[:, 0]
    row_x, row_z = codes[:, :XROWS].reshape(-1), codes[:, XROWS : XROWS + ZROWS]

    meta = jnp.stack([row_x // CODE // n_row, row_x % CODE // n_col])
    meta = jnp.where(row_x >= 0, meta, -1).astype(tiles.dtype).reshape(-1, LANES)
    meta = jnp.pad(meta, ((0, META - meta.shape[0]), (0, 0)))
    labelled = jnp.concatenate([tiles.reshape(-1, LANES), meta])
    col_tiles = send_all(labelled, "row", n_row // CORES, axis_index_groups=core_groups)
    other = lax.ppermute(col_tiles, "row", [(n, n ^ 1) for n in range(n_row)])
    core = lax.axis_index("row") % CORES
    col_tiles = jnp.concatenate([col_tiles, other])
    n_codes = n_col * XROWS
    all_x = col_tiles[:, -META : -META + 2 * n_codes // LANES].astype(jnp.float32)
    all_x = all_x.reshape(CORES, n_row // CORES, 2, n_col, XROWS)
    device = jnp.arange(n_row // CORES) * CORES
    device = jnp.stack([device + core, device + 1 - core]).astype(jnp.float32)

    col_x = lax.dynamic_index_in_dim(all_x, col, 3, keepdims=False)
    col_x = jnp.stack(
        [col_x[:, :, 0] * n_row + device[:, :, None], col_x[:, :, 1] * n_col + col]
    )
    own_places = lax.dynamic_index_in_dim(all_x, col, 3, keepdims=False)[:, :, 0]
    col_x = jnp.where(own_places >= 0, col_x, -1.0).reshape(2, -1)

    row_z_padded = jnp.pad(row_z, ((0, 0), (0, ZSTEP - ZROWS)), constant_values=-1)

    def table(rows):
        return jax.ShapeDtypeStruct((rows, LANES), jnp.int32)

    row_codes = decode(row_x)
    square_list, cube_list = call(
        match_kernel,
        (),
        (
            sublanes(decode(z_codes)),
            sublanes(decode(x_codes)),
            row_codes,
            decode(row_z_padded.reshape(-1)),
            col_x,
        ),
        (table(ZROWS), table(XROWS)),
    )

    start = far_own * NEAR % n_row // CORES
    cross = lax.dynamic_slice_in_dim(all_x, start, NEAR // CORES, 1)
    rows = lax.dynamic_slice_in_dim(device, start, NEAR // CORES, 1)
    in_order = core == 0
    cross = jnp.where(in_order, cross, cross[::-1]).transpose(1, 0, 2, 3, 4)
    rows = jnp.where(in_order, rows, rows[::-1]).transpose(1, 0).reshape(NEAR, 1, 1)
    cross = cross.reshape(NEAR, 2, n_col, XROWS)
    device = jnp.arange(n_col)[:, None]
    cross_k = cross[:, 0] * n_row + rows
    cross_j = cross[:, 1] * n_col + device.astype(jnp.float32)
    cross_k = jnp.where((cross[:, 0] >= 0) & (device % NEAR == near_own), cross_k, -1.0)
    cross_y = jnp.broadcast_to((device // NEAR).astype(jnp.float32), cross_j.shape)
    cross_x = jnp.stack([cross_k, cross_j, cross_y], axis=1).reshape(NEAR, 3, -1)
    near_z = lax.dynamic_slice_in_dim(row_z, far_own * NEAR, NEAR, 0).reshape(-1)
    send_list, loads = call(
        send_kernel,
        (),
        (sublanes(decode(near_z)), row_codes, cross_x),
        (table(NEAR * ZROWS), table(1)),
    )
    square = call(
        square_kernel,
        (square_list,),
        (row_tiles, col_tiles),
        jax.ShapeDtypeStruct((NEAR, z_rows.shape[0] // 2, size, LANES), jnp.bfloat16),
        sums_scratch(ZROWS),
    )
    near = lax.all_to_all(
        square, "col", split_axis=0, concat_axis=0, axis_index_groups=near_groups
    )

    def one_round(first, base, count):
        info = jnp.stack([first, far_own])
        packed = call(
            pack_kernel,
            (info, loads, send_list),
            (near,),
            jax.ShapeDtypeStruct((n_far, count * size + META, LANES), jnp.bfloat16),
        )
        far = lax.all_to_all(
            packed, "col", split_axis=0, concat_axis=0, axis_index_groups=far_groups
        )
        return call(
            cube_kernel,
            (info, cube_list),
            (near, far, col_tiles, base),
            (
                jax.ShapeDtypeStruct(base.shape, jnp.float32),
                jax.ShapeDtypeStruct((1,), jnp.int32),
            ),
            sums_scratch(XROWS),
        )

    def next_round(state):
        first, base, _ = state
        return (first + 2 * MORE, *one_round(first, base, MORE))

    used = jnp.repeat((x_rows >= 0).astype(jnp.float32), size)
    base = 1.5 * own.astype(jnp.float32) * used[None]
    state = (jnp.int32(2 * FIRST), *one_round(jnp.int32(0), base, FIRST))
    _, result, _ = lax.while_loop(lambda state: state[0] < state[2][0], next_round, state)
    return result[None, None]


def solution(mesh):
    placed = (
        P("row", "col", None, None),
        P("row", "col", None),
        P("row", "col", None),
        P("row", "col", None),
        P("row", "col", None),
    )
    return jax.shard_map(
        per_device,
        mesh=mesh,
        in_specs=placed,
        out_specs=P("row", "col", None, None),
        check_vma=False,
    )
```

time: 346 us -> 171 us (0.49)
  blocking collectives: 152 us -> 28.5 us
  local copies, waits for them, and re-layouts: 104 us -> 8.7 us
  starting transfers between devices: 0.08 us -> 23.3 us
  Pallas kernels: 0 us -> 22.5 us
  waiting for transfers between devices: 54.8 us -> 70.4 us
  other arithmetic: 14.4 us -> 0.7 us
  matrix products: 6.17 us -> 0 us
    all_gather x6 -> x0, blocking collectives: 152 us -> none  [the longest x1 29.4 us: per_device(): lax.all_gather(x_rows, 'col', axis=1, tiled=True)]
    all_to_all x0 -> x3, waiting for transfers between devices: none -> 69.1 us  [the longest x1 39.1 us: one_round(): lax.all_to_all(packed, 'col', split_axis=0, concat_axis=0, axis_index_gro...]
    all_gather x3 -> x1, waiting for transfers between devices: 53.4 us -> 0.02 us  [per_device(): lax.all_gather(near_tiles, 'col', axis=0, axis_index_groups=far_groups)]
    another operation x4 -> x7, local copies, waits for them, and re-layouts: 44.9 us -> 1.43 us  [the longest x1 1.06 us: per_device(): tiles = own.reshape(size, width // LANES, LANES).transpose(1, 0, 2)]
    transpose x3, local copies, waits for them, and re-layouts: 30 us -> 0.2 us  [the longest x1 0.09 us: per_device(): jnp.where(in_order, rows, rows[::-1]).transpose(1, 0).reshape(NEAR, 1, 1)]
    all_to_all x0 -> x2, blocking collectives: none -> 28.5 us  [send_all(): return lax.all_to_all(copies, axis, split_axis=0, concat_axis=0, **groups)]
    gather x8 -> x0, local copies, waits for them, and re-layouts: 24.8 us -> none  [the longest x2 13.3 us: pick_blocks(): taken = piece_blocks[where_index]]
    pallas_call x0 -> x5, Pallas kernels: none -> 22.5 us  [call(): pl.pallas_call(kernel, out_shape=out, in_specs=[SMEM] * len(scalars) + [V...]
  transfers between devices with their start and end apart: 3 -> 5, of which waited for: 2 -> 4; matrix products, arithmetic and copies ran while one was open for 11% -> 3% of each run, Pallas kernels for 0% -> 5%
where the time goes in v1:
time: 171 us; the launch traced here: 168 us
  waiting for transfers between devices  70.4 us (41%)
  blocking collectives  28.5 us (17%)
  starting transfers between devices  23.3 us (14%)
  Pallas kernels  22.5 us (13%)
  between operations  13.8 us (8%)
  local copies, waits for them, and re-layouts  8.7 us (5%)
    all_to_all x1, waiting for transfers between devices, one_round(): lax.all_to_all(packed, 'col', split_axis=0, concat_axis=0, axis_index_gro...  39.1 us
    all_to_all x2, blocking collectives, send_all(): return lax.all_to_all(copies, axis, split_axis=0, concat_axis=0, **groups)  28.5 us
    all_to_all x1, waiting for transfers between devices, send_all(): return lax.all_to_all(copies, axis, split_axis=0, concat_axis=0, **groups)  23.3 us
    pallas_call x5, Pallas kernels, call(): pl.pallas_call(kernel, out_shape=out, in_specs=[SMEM] * len(scalars) + [V...  22.5 us
    all_to_all x1, starting transfers between devices, send_all(): return lax.all_to_all(copies, axis, split_axis=0, concat_axis=0, **groups)  10 us
    all_to_all x1, waiting for transfers between devices, per_device(): lax.all_to_all(square, 'col', split_axis=0, concat_axis=0, axis_index_gro...  6.77 us
    ppermute x1, starting transfers between devices, per_device(): other = lax.ppermute(col_tiles, 'row', [(n, n ^ 1) for n in range(n_row)])  5.94 us
    all_to_all x1, starting transfers between devices, one_round(): lax.all_to_all(packed, 'col', split_axis=0, concat_axis=0, axis_index_gro...  3.71 us
  transfers between devices with their start and end apart: 5, of which 4 were waited for; matrix products, arithmetic and copies ran while one was open for 3% of the time, Pallas kernels for 5%

profile of v1, /device:TPU:1, one launch (start us, length us, event | category | flops | bytes accessed | tf_op | source)
XLA Modules:
  0.0 168.5 jit_solution(17899592429358139760)
XLA Ops:
  6.6 1.1 reshape_squeeze.3
  7.7 0.1 broadcast_in_dim.87
  7.8 11.3 %all_to_all.31 = bf16[4,7,64,128]{3,2,1,0:T(8,128)(2,1)} all-to-all(bf16[4,7,64,128]{3,2,1,0:T(8,128)(2,1)S(1)} %broadcast_in_dim.87), channel_id=1, replica_groups={{0,1,2,3},{4,5,6,7},{8,9,10,11},{12,13,14,15},{16,17,18,19},{20,21,22,2..., dimensions={0} | all-to-all | bytes 917504 | tf_op jit(solution)/shard_map/all_to_all | solution.py:330
  19.3 17.2 %all_to_all.32 = s32[32,1,128]{2,1,0:T(1,128)S(1)} all-to-all(s32[32,1,128]{2,1,0:T(1,128)S(1)} %broadcast_in_dim.88), channel_id=1, replica_groups=mesh['row'=16,'col'=32] {'col'}, dimensions={0} | all-to-all | bytes 32768 | tf_op jit(solution)/shard_map/all_to_all | solution.py:330
  36.7 0.1 ge.101
  36.8 1.1 broadcast_in_dim.92
  37.9 10.0 %all-to-all-start.3 = ((bf16[8,464,128]{2,1,0:T(8,128)(2,1)}), bf16[8,464,128]{2,1,0:T(8,128)(2,1)S(1)}, u32[]{:S(2)}, u32[]{:S(2)}) async-start(bf16[8,464,128]{2,1,0:T(8,128)(2,1)} %broadcast_in_dim.92), calls=%async_computation.3 | async-start | bytes 1900544 | tf_op jit(solution)/shard_map/all_to_all | solution.py:330
  48.2 23.3 %all-to-all-done.3 = bf16[8,464,128]{2,1,0:T(8,128)(2,1)S(1)} async-done(((bf16[8,464,128]{2,1,0:T(8,128)(2,1)}), bf16[8,464,128]{2,1,0:T(8,128)(2,1)S(1)}, u32[]{:S(2)}, u32[]{:S(2)}) %all-to-all-start.3) | async-done | bytes 950304 | tf_op jit(solution)/shard_map/all_to_all | solution.py:330
  71.5 5.9 %collective-permute-start = (bf16[8,464,128]{2,1,0:T(8,128)(2,1)S(1)}, bf16[8,464,128]{2,1,0:T(8,128)(2,1)}, u32[]{:S(2)}, u32[]{:S(2)}) collective-permute-start(bf16[8,464,128]{2,1,0:T(8,128)(2,1)S(1)} %all-to-all-done.3), channel_id=1, source_target_pairs={{0,32},{32,0},{64,96},{96,64},{128,160},{160,128},{192,224},{224,1... | collective-permute-start | bytes 2850824 | tf_op jit(solution)/shard_map/ppermute | solution.py:362
  77.5 0.1 copy.29
  77.6 0.1 add.273
  78.1 0.1 reshape.732
  78.5 1.3 collective-permute-done
  79.7 1.3 constant_dynamic-update-slice_fusion.col_tiles
  81.1 0.2 reshape.735
  81.5 0.1 ge.104
  81.7 1.5 shard_map.55
  83.3 2.0 %copy-done = bf16[32,7,64,128]{3,2,1,0:T(8,128)(2,1)S(1)} copy-done((bf16[32,7,64,128]{3,2,1,0:T(8,128)(2,1)S(1)}, bf16[32,7,64,128]{3,2,1,0:T(8,128)(2,1)}, u32[]{:S(2)}) %copy-start) | copy-done | bytes 3670040
  85.3 4.7 %shard_map.56 = bf16[4,18,64,128]{3,2,1,0:T(8,128)(2,1)} custom-call(s32[40,128]{1,0:T(8,128)S(1)} %get-tuple-element.63.lists, bf16[32,7,64,128]{3,2,1,0:T(8,128)(2,1)S(1)} %copy-done, bf16[16,464,128]{2,1,0:T(8,128)(2,1)S(1)} %constant_dynamic-update-slice_fusion.col_tiles), custom_call_target="tpu_custom_call" | custom-call | tf_op jit(solution)/shard_map/pallas_call | solution.py:296
  90.0 3.5 %all-to-all-start.4 = ((bf16[4,18,64,128]{3,2,1,0:T(8,128)(2,1)}), bf16[4,18,64,128]{3,2,1,0:T(8,128)(2,1)S(1)}, u32[]{:S(2)}, u32[]{:S(2)}) async-start(bf16[4,18,64,128]{3,2,1,0:T(8,128)(2,1)} %shard_map.56), calls=%async_computation.4 | async-start | bytes 2359296 | tf_op jit(solution)/shard_map/all_to_all | solution.py:424
  93.7 0.1 copy.28
  93.9 0.1 stack.92
  94.1 0.1 stack.93
  94.2 0.1 broadcast_in_dim.95.near_z
  94.3 6.7 %shard_map.57 = (s32[160,128]{1,0:T(8,128)S(1)}, s32[1,128]{1,0:T(1,128)S(1)}) custom-call(f32[2,160,128]{2,1,0:T(8,128)S(1)} %broadcast_in_dim.95.near_z, f32[2,512]{1,0:T(2,128)S(1)} %get-tuple-element.107.row_x, f32[4,3,512]{2,1,0:T(4,128)S(1)} %pad_maximum_fusion.cross_x), custom_call_target="tpu_custom_call" | custom-call | tf_op jit(solution)/shard_map/pallas_call | solution.py:296
  101.0 6.8 %all-to-all-done.4.near = bf16[4,18,64,128]{3,2,1,0:T(8,128)(2,1)S(1)} async-done(((bf16[4,18,64,128]{3,2,1,0:T(8,128)(2,1)}), bf16[4,18,64,128]{3,2,1,0:T(8,128)(2,1)S(1)}, u32[]{:S(2)}, u32[]{:S(2)}) %all-to-all-start.4) | async-done | bytes 1179680 | tf_op jit(solution)/shard_map/all_to_all | solution.py:424
  107.8 5.0 %shard_map.58 = bf16[8,784,128]{2,1,0:T(8,128)(2,1)} custom-call(s32[2]{0:T(128)S(1)} %pad_add_fusion.2.info, s32[1,128]{1,0:T(1,128)S(1)} %get-tuple-element.173.loads, s32[160,128]{1,0:T(8,128)S(1)} %get-tuple-element.174.lists, bf16[4,18,64,128]{3,2,1,0:T(8,128)(2,1)S(1)} %all-to-all-done.4.near), custom_call_target="tpu_custom_call" | custom-call | tf_op jit(solution)/shard_map/pallas_call | solution.py:296
  112.8 3.7 %all-to-all-start.5 = ((bf16[8,784,128]{2,1,0:T(8,128)(2,1)}), bf16[8,784,128]{2,1,0:T(8,128)(2,1)S(1)}, u32[]{:S(2)}, u32[]{:S(2)}) async-start(bf16[8,784,128]{2,1,0:T(8,128)(2,1)} %shard_map.58), calls=%async_computation.5 | async-start | bytes 3211264 | tf_op jit(solution)/shard_map/all_to_all | solution.py:436
  116.7 39.1 %all-to-all-done.5.far = bf16[8,784,128]{2,1,0:T(8,128)(2,1)S(1)} async-done(((bf16[8,784,128]{2,1,0:T(8,128)(2,1)}), bf16[8,784,128]{2,1,0:T(8,128)(2,1)S(1)}, u32[]{:S(2)}, u32[]{:S(2)}) %all-to-all-start.5) | async-done | bytes 1605664 | tf_op jit(solution)/shard_map/all_to_all | solution.py:436
  155.7 4.6 %shard_map.59 = (f32[64,896]{1,0:T(8,128)S(1)}, s32[1]{0:T(128)}) custom-call(s32[2]{0:T(128)S(1)} %pad_add_fusion.2.info, s32[16,128]{1,0:T(8,128)S(1)} %get-tuple-element.176.lists, bf16[4,18,64,128]{3,2,1,0:T(8,128)(2,1)S(1)} %all-to-all-done.4.near, bf16[8,784,128]{2,1,0:T(8,128)(2,1)S(1)} %all-to-all-done.5.far, bf16[16,464,128]{2,1,0:T(8,128)(2,1)} %copy-done.1, ...), custom_call_target="tpu_custom_call" | custom-call | tf_op jit(solution)/shard_map/pallas_call | solution.py:296
  160.4 0.6 while.12
  161.0 0.7 copy-done.2
  (80 shorter events, 2.2 us)
Async XLA Ops:
  6.5 12.6 %copy-start.7 = (s32[1,1,14]{2,1,0:T(1,128)S(1)}, s32[1,1,14]{2,1,0:T(1,128)}, u32[]{:S(2)}) copy-start(s32[1,1,14]{2,1,0:T(1,128)} %param.8) | copy-start | bytes 172
  6.5 12.6 %copy-start.4 = (s32[1,1,14]{2,1,0:T(1,128)S(1)}, s32[1,1,14]{2,1,0:T(1,128)}, u32[]{:S(2)}) copy-start(s32[1,1,14]{2,1,0:T(1,128)} %param.9) | copy-start | bytes 172
  6.5 12.6 %copy-start.5 = (s32[1,1,36]{2,1,0:T(1,128)S(1)}, s32[1,1,36]{2,1,0:T(1,128)}, u32[]{:S(2)}) copy-start(s32[1,1,36]{2,1,0:T(1,128)} %param.10) | copy-start | bytes 436
  6.5 12.7 %copy-start.6 = (s32[1,1,36]{2,1,0:T(1,128)S(1)}, s32[1,1,36]{2,1,0:T(1,128)}, u32[]{:S(2)}) copy-start(s32[1,1,36]{2,1,0:T(1,128)} %param.11) | copy-start | bytes 436
  6.5 76.7 %all-gather.3.cloned.1.call-start = ((), (), s32[]{:S(2)}) async-start(), calls=%async_computation.6 | async-start | bytes 4128768 | tf_op jit(solution)/shard_map/all_gather | solution.py:347
  37.9 33.6 %all-to-all-start.3 = ((bf16[8,464,128]{2,1,0:T(8,128)(2,1)}), bf16[8,464,128]{2,1,0:T(8,128)(2,1)S(1)}, u32[]{:S(2)}, u32[]{:S(2)}) async-start(bf16[8,464,128]{2,1,0:T(8,128)(2,1)} %broadcast_in_dim.92), calls=%async_computation.3 | async-start | bytes 1900544 | tf_op jit(solution)/shard_map/all_to_all | solution.py:330
  71.5 8.2 %collective-permute-start = (bf16[8,464,128]{2,1,0:T(8,128)(2,1)S(1)}, bf16[8,464,128]{2,1,0:T(8,128)(2,1)}, u32[]{:S(2)}, u32[]{:S(2)}) collective-permute-start(bf16[8,464,128]{2,1,0:T(8,128)(2,1)S(1)} %all-to-all-done.3), channel_id=1, source_target_pairs={{0,32},{32,0},{64,96},{96,64},{128,160},{160,128},{192,224},{224,1... | collective-permute-start | bytes 2850824 | tf_op jit(solution)/shard_map/ppermute | solution.py:362
  81.0 9.0 %copy-start.1 = (bf16[16,464,128]{2,1,0:T(8,128)(2,1)}, bf16[16,464,128]{2,1,0:T(8,128)(2,1)S(1)}, u32[]{:S(2)}) copy-start(bf16[16,464,128]{2,1,0:T(8,128)(2,1)S(1)} %constant_dynamic-update-slice_fusion.col_tiles) | copy-start | bytes 5701636
  83.3 2.0 %copy-start = (bf16[32,7,64,128]{3,2,1,0:T(8,128)(2,1)S(1)}, bf16[32,7,64,128]{3,2,1,0:T(8,128)(2,1)}, u32[]{:S(2)}) copy-start(bf16[32,7,64,128]{3,2,1,0:T(8,128)(2,1)} %all-gather.3.cloned.1.call-done.row_tiles) | copy-start | bytes 11010052
  90.0 17.8 %all-to-all-start.4 = ((bf16[4,18,64,128]{3,2,1,0:T(8,128)(2,1)}), bf16[4,18,64,128]{3,2,1,0:T(8,128)(2,1)S(1)}, u32[]{:S(2)}, u32[]{:S(2)}) async-start(bf16[4,18,64,128]{3,2,1,0:T(8,128)(2,1)} %shard_map.56), calls=%async_computation.4 | async-start | bytes 2359296 | tf_op jit(solution)/shard_map/all_to_all | solution.py:424
  112.8 3.9 %copy-start.3 = (bf16[1,1,64,896]{3,2,1,0:T(8,128)(2,1)S(1)}, bf16[1,1,64,896]{3,2,1,0:T(8,128)(2,1)}, u32[]{:S(2)}) copy-start(bf16[1,1,64,896]{3,2,1,0:T(8,128)(2,1)} %param.7) | copy-start | bytes 344068
  112.8 43.0 %all-to-all-start.5 = ((bf16[8,784,128]{2,1,0:T(8,128)(2,1)}), bf16[8,784,128]{2,1,0:T(8,128)(2,1)S(1)}, u32[]{:S(2)}, u32[]{:S(2)}) async-start(bf16[8,784,128]{2,1,0:T(8,128)(2,1)} %shard_map.58), calls=%async_computation.5 | async-start | bytes 3211264 | tf_op jit(solution)/shard_map/all_to_all | solution.py:436
  161.0 0.7 copy-start.2
Sparse Core Ops, SparseCore 0:
  19.3 57.4 all-gather.2

commit v2 on v1

--- a/solution.py
+++ b/solution.py
@@ -8,6 +8,7 @@
 from jax.sharding import PartitionSpec as P
 
 NEIGH = 7
+CODE = 512
 CORES = 2
 NEAR = 4
 XROWS = 16
@@ -17,14 +18,13 @@
 FIRST = 12
 MORE = 2
 META = 16
-CODE = 512
 LANES = 128
 CHUNK = 2
 GROUP = 8
 STEP = 2
 COUNT = 32
 FAR = 1e9
-PARAMS = pltpu.CompilerParams(vmem_limit_bytes=20 * 1024 * 1024)
+MIB = 1024 * 1024
 VMEM = pl.BlockSpec(memory_space=pltpu.VMEM)
 SMEM = pl.BlockSpec(memory_space=pltpu.SMEM)
 
@@ -33,6 +33,10 @@
     return lax.broadcasted_iota(jnp.int32, (1, width), 1).astype(jnp.float32)
 
 
+def beside(*refs):
+    return (jnp.concatenate([ref[n : n + 1, :] for ref in refs], axis=1) for n in range(2))
+
+
 def following(hits, lanes, last):
     return jnp.min(jnp.where(hits & (lanes > last), lanes, FAR), axis=1, keepdims=True)
 
@@ -45,9 +49,9 @@
     return jnp.where((lane_numbers(LANES) == base + count) & good, value, table)
 
 
-def match_kernel(own_z, own_x, row_x, row_z, col_x, square_list, cube_list):
+def square_match(own_z, row_x, own_col, other_col, square_list):
     row_i, row_m = row_x[0:1, :], row_x[1:2, :]
-    col_m, col_k = col_x[0:1, :], col_x[1:2, :]
+    col_m, col_k = beside(own_col, other_col)
     row_lanes, col_lanes = lane_numbers(row_i.shape[1]), lane_numbers(col_m.shape[1])
     lane = lane_numbers(LANES)
 
@@ -66,6 +70,9 @@
         count = count + jnp.where(good, 1.0, 0.0)
     square_list[...] = jnp.where(lane == COUNT, count, table).astype(jnp.int32)
 
+def cube_match(here, own_x, row_z, own_col, other_col, near_list, far_list):
+    col_m, col_k = beside(own_col, other_col)
+    col_lanes, lane = lane_numbers(col_m.shape[1]), lane_numbers(LANES)
     z_lanes = lane_numbers(row_z.shape[1])
     z_i, z_k = row_z[0:1, :], row_z[1:2, :]
     i, j = own_x[0][:, :1], own_x[1][:, :1]
@@ -89,21 +96,28 @@
         < lax.broadcasted_iota(jnp.int32, (SEGMENT, SEGMENT), 1)
     ).astype(jnp.float32)
     rank = jnp.dot(needed, before, preferred_element_type=jnp.float32)
+    n_groups = rank.shape[0]
     rank = jnp.concatenate([rank[n : n + 1] for n in range(rank.shape[0])], axis=1)
-    table = jnp.zeros((XROWS, LANES), jnp.float32)
-    count = jnp.zeros((XROWS, 1), jnp.float32)
-    for last, entry in entries:
-        good = entry >= 0
-        place = picked(z_lanes == entry, rank)
-        group = jnp.floor(entry / SEGMENT)
-        value = (group * SEGMENT + place) * SEGMENT + entry - group * SEGMENT
-        table = put(table, 0, count, good, value)
-        table = put(table, 8, count, good, last)
-        count = count + jnp.where(good, 1.0, 0.0)
-    cube_list[...] = jnp.where(lane == COUNT, count, table).astype(jnp.int32)
-
-
-def send_kernel(near_z, row_x, cross_x, send_list, loads):
+    own = here[0].astype(jnp.float32)
+    for near, out_ref in ((True, near_list), (False, far_list)):
+        table = jnp.zeros((XROWS, LANES), jnp.float32)
+        count = jnp.zeros((XROWS, 1), jnp.float32)
+        for last, entry in entries:
+            group = jnp.floor(entry / SEGMENT)
+            entry_of = entry - group * SEGMENT
+            if near:
+                good = (entry >= 0) & (group == own)
+                value = entry_of
+            else:
+                good = (entry >= 0) & (group != own)
+                value = picked(z_lanes == entry, rank) * n_groups + group
+            table = put(table, 0, count, good, value)
+            table = put(table, 8, count, good, last)
+            count = count + jnp.where(good, 1.0, 0.0)
+        out_ref[...] = jnp.where(lane == COUNT, count, table).astype(jnp.int32)
+
+
+def send_kernel(near_z, row_x, cross_x, send_list, loads, ranked):
     row_i, row_m = row_x[0:1, :], row_x[1:2, :]
     row_lanes, lane = lane_numbers(row_i.shape[1]), lane_numbers(LANES)
     needs, numbers = [], []
@@ -135,10 +149,12 @@
     def list_rank(p, carry):
         at = rank == p.astype(jnp.float32)
         row = jnp.sum(jnp.where(at, number, 0.0), axis=0, keepdims=True)
-        send_list[pl.ds(p, 1), :] = row.astype(jnp.int32)
+        ranked[pl.ds(p, 1), :] = row
         return carry
 
+    ranked[...] = jnp.zeros_like(ranked)
     lax.fori_loop(0, size, list_rank, 0)
+    send_list[...] = ranked[...].T[: send_list.shape[0], :].astype(jnp.int32)
     loads[...] = jnp.sum(need, axis=0, keepdims=True).astype(jnp.int32)
 
 
@@ -163,7 +179,7 @@
     return jnp.where(lane < 64, even, odd)
 
 
-def add_products(lists, rows, load_left, load_right, sums, chunks):
+def add_products(lists, rows, load_left, load_right, sums, chunks, wait=None):
     sums[...] = jnp.zeros_like(sums)
 
     def per_row(n, length):
@@ -176,6 +192,8 @@
     length = lax.fori_loop(0, rows - 1, per_row, 0)
     for spare in range(GROUP):
         chunks[length + spare] = (rows - 1) << 3
+    if wait is not None:
+        wait()
 
     def per_group(group, carry):
         values = []
@@ -207,19 +225,27 @@
     return ref.at[pl.ds(pl.multiple_of(tile * 64, 64), 64), :]
 
 
-def x_tile(ref, entry):
+def x_tile(own, other, entry):
     device, tile, half = tile_of(entry, XROWS)
-    return rows_of(ref.at[device], tile)[...] * half_mask(half, 1)
-
-
-def square_kernel(lists, row_tiles, col_tiles, out_ref, sums, chunks):
+    shift = own.shape[0].bit_length() - 1
+    core, device = device >> shift, device & (own.shape[0] - 1)
+    tiles = (rows_of(ref.at[device], tile)[...] for ref in (own, other))
+    own_tile, other_tile = tiles
+    return own_tile * half_mask(half, 1 - core) + other_tile * half_mask(half, core)
+
+
+def square_kernel(
+    lists, row_hbm, own_tiles, other_tiles, out_ref, sums, chunks, row_tiles, arrived
+):
+    fetch = pltpu.make_async_copy(row_hbm, row_tiles, arrived)
+    fetch.start()
+
     def load_left(entry, good):
         device, tile, half = tile_of(entry, XROWS)
-        return row_tiles[device, tile] * half_mask(half, good)
-
-    add_products(
-        lists, ZROWS, load_left, functools.partial(x_tile, col_tiles), sums, chunks
-    )
+        return rows_of(row_tiles.at[device], tile)[...] * half_mask(half, good)
+
+    load_right = functools.partial(x_tile, own_tiles, other_tiles)
+    add_products(lists, ZROWS, load_left, load_right, sums, chunks, fetch.wait)
 
     def store(n, carry):
         square = pair_up(sums[2 * n], sums[2 * n + 1]).astype(jnp.bfloat16)
@@ -250,7 +276,7 @@
                 for half in range(2):
                     place = step * (2 * STEP) + 2 * n + half
                     good = (place < number).astype(jnp.int32)
-                    entry = lists[jnp.minimum(first + place, lists.shape[0] - 1), target]
+                    entry = lists[target, jnp.minimum(first + place, lists.shape[1] - 1)]
                     device, tile, side = tile_of(entry, ZSTEP)
                     both.append(to_half(near[device, tile], side, half) * half_mask(half, good))
                 packed.append(both[0] + both[1])
@@ -263,43 +289,56 @@
     lax.fori_loop(0, out_ref.shape[0], per_target, 0)
 
 
-def cube_kernel(info, lists, near, far, col_tiles, base, out_ref, most_ref, sums, chunks):
-    first, own = info[0], info[1]
-    places = (far.shape[1] - META) // 32
-    most = far[0, places * 32 :, :]
-    for n in range(1, far.shape[0]):
-        most = jnp.maximum(most, far[n, places * 32 :, :])
-    most_ref[0] = jnp.max(most.astype(jnp.float32)).astype(jnp.int32)
-
-    def load_left(code, good):
-        group, rank, entry = code >> 16, (code >> 8) & 255, code & 255
-        here = group == own
-        close = good * (here & (first == 0)).astype(jnp.int32)
-        place = rank - first
-        inside = (place >= 0) & (place < places) & ~here
-        away = good * inside.astype(jnp.int32)
-        place = jnp.clip(place, 0, places - 1)
-        device, tile, half = tile_of(entry, ZSTEP)
-        left = near[device, tile] * half_mask(half, close)
-        return left + rows_of(far.at[group], place >> 1)[...] * half_mask(place & 1, away)
-
-    add_products(
-        lists, XROWS, load_left, functools.partial(x_tile, col_tiles), sums, chunks
-    )
+def subtract_cubes(sums, base, out_ref):
     for n in range(out_ref.shape[1] // LANES):
         here = slice(n * LANES, (n + 1) * LANES)
         out_ref[:, here] = base[:, here] - 0.5 * pair_up(sums[2 * n], sums[2 * n + 1])
 
 
-def call(kernel, scalars, arrays, out, scratch=()):
+def near_kernel(lists, near, own_tiles, other_tiles, base, out_ref, sums, chunks):
+    def load_left(entry, good):
+        device, tile, half = tile_of(entry, ZSTEP)
+        return near[device, tile] * half_mask(half, good)
+
+    load_right = functools.partial(x_tile, own_tiles, other_tiles)
+    add_products(lists, XROWS, load_left, load_right, sums, chunks)
+    subtract_cubes(sums, base, out_ref)
+
+
+def far_kernel(
+    info, lists, far, own_tiles, other_tiles, base, out_ref, most_ref, sums, chunks
+):
+    first = info[0]
+    n_groups = far.shape[0]
+    shift = n_groups.bit_length() - 1
+    places = (far.shape[1] - META) // 32
+    most = far[0, places * 32 :, :]
+    for n in range(1, n_groups):
+        most = jnp.maximum(most, far[n, places * 32 :, :])
+    most_ref[0] = jnp.max(most.astype(jnp.float32)).astype(jnp.int32)
+
+    def load_left(code, good):
+        group, place = code & (n_groups - 1), (code >> shift) - first
+        good = good * ((place >= 0) & (place < places)).astype(jnp.int32)
+        place = jnp.clip(place, 0, places - 1)
+        return rows_of(far.at[group], place >> 1)[...] * half_mask(place & 1, good)
+
+    load_right = functools.partial(x_tile, own_tiles, other_tiles)
+    add_products(lists, XROWS, load_left, load_right, sums, chunks)
+    subtract_cubes(sums, base, out_ref)
+
+
+def call(kernel, scalars, arrays, out, scratch=(), far_off=0):
     single = isinstance(out, jax.ShapeDtypeStruct)
     return pl.pallas_call(
         kernel,
         out_shape=out,
-        in_specs=[SMEM] * len(scalars) + [VMEM] * len(arrays),
+        in_specs=[SMEM] * len(scalars)
+        + [pl.BlockSpec(memory_space=pl.ANY)] * far_off
+        + [VMEM] * (len(arrays) - far_off),
         out_specs=VMEM if single else [SMEM if o.shape == (1,) else VMEM for o in out],
         scratch_shapes=scratch,
-        compiler_params=PARAMS,
+        compiler_params=pltpu.CompilerParams(vmem_limit_bytes=(58 if far_off else 20) * MIB),
     )(*scalars, *arrays)
 
 
@@ -310,15 +349,14 @@
     ]
 
 
-def decode(codes):
-    rows = jnp.where(codes >= 0, codes // CODE, -1)
-    cols = jnp.where(codes >= 0, codes % CODE, -1)
-    return jnp.stack([rows, cols]).astype(jnp.float32)
-
-
-def encode(rows, cols, length):
-    codes = jnp.where(rows >= 0, rows * CODE + cols, -1)
-    return jnp.pad(codes, (0, length - codes.shape[0]), constant_values=-1)
+def numbers(found, n_row, row, n_col, col):
+    lines = jnp.stack([found[0] * n_row + row, found[1] * n_col + col])
+    return jnp.where(found[0] >= 0, lines, -1.0)
+
+
+def listed(rows, cols, length):
+    lines = jnp.stack([rows, cols])
+    return jnp.pad(lines, ((0, 0), (0, length - rows.shape[0])), constant_values=-1)
 
 
 def sublanes(pairs):
@@ -342,84 +380,92 @@
     far_groups = [[y * NEAR + x for y in range(n_far)] for x in range(NEAR)]
     core_groups = [[z + core for z in range(0, n_row, CORES)] for core in range(CORES)]
 
-    tiles = own.reshape(size, width // LANES, LANES).transpose(1, 0, 2)
+    row = lax.axis_index("row")
+
+    tiles = own.reshape(size, width // LANES, LANES).transpose(1, 0, 2).reshape(-1, LANES)
     near_tiles = send_all(tiles, "col", NEAR, axis_index_groups=near_groups)
     row_tiles = lax.all_gather(near_tiles, "col", axis=0, axis_index_groups=far_groups)
-    row_tiles = row_tiles.reshape(n_col, *tiles.shape)
-
-    x_codes, z_codes = encode(x_rows, x_cols, XROWS), encode(z_rows, z_cols, ZROWS)
-    codes = jnp.concatenate([x_codes, z_codes])
+    row_tiles = row_tiles.reshape(n_col, -1, LANES)
+
+    own_x, own_z = listed(x_rows, x_cols, XROWS), listed(z_rows, z_cols, ZROWS)
+    codes = jnp.concatenate([own_x, own_z], axis=1)
+    codes = jnp.where(codes[0] >= 0, codes[0] * CODE + codes[1], -1)
     codes = jnp.pad(codes, (0, LANES - codes.shape[0]), constant_values=-1)
     codes, near_tiles = lax.optimization_barrier((codes, near_tiles))
     codes = send_all(codes[None], "col", n_col)[:, 0]
-    row_x, row_z = codes[:, :XROWS].reshape(-1), codes[:, XROWS : XROWS + ZROWS]
-
-    meta = jnp.stack([row_x // CODE // n_row, row_x % CODE // n_col])
-    meta = jnp.where(row_x >= 0, meta, -1).astype(tiles.dtype).reshape(-1, LANES)
+    lines = jnp.where(codes >= 0, jnp.stack([codes // CODE, codes % CODE]), -1)
+    row_x = lines[:, :, :XROWS].reshape(2, -1).astype(jnp.float32)
+    row_z = lines[:, :, XROWS : XROWS + ZROWS].astype(jnp.float32)
+
+    meta = jnp.stack([codes // CODE // n_row, codes % CODE // n_col])
+    meta = jnp.where(codes >= 0, meta, -1)[:, :, :XROWS].astype(own.dtype).reshape(-1, LANES)
     meta = jnp.pad(meta, ((0, META - meta.shape[0]), (0, 0)))
-    labelled = jnp.concatenate([tiles.reshape(-1, LANES), meta])
-    col_tiles = send_all(labelled, "row", n_row // CORES, axis_index_groups=core_groups)
-    other = lax.ppermute(col_tiles, "row", [(n, n ^ 1) for n in range(n_row)])
-    core = lax.axis_index("row") % CORES
-    col_tiles = jnp.concatenate([col_tiles, other])
-    n_codes = n_col * XROWS
-    all_x = col_tiles[:, -META : -META + 2 * n_codes // LANES].astype(jnp.float32)
-    all_x = all_x.reshape(CORES, n_row // CORES, 2, n_col, XROWS)
-    device = jnp.arange(n_row // CORES) * CORES
-    device = jnp.stack([device + core, device + 1 - core]).astype(jnp.float32)
-
-    col_x = lax.dynamic_index_in_dim(all_x, col, 3, keepdims=False)
-    col_x = jnp.stack(
-        [col_x[:, :, 0] * n_row + device[:, :, None], col_x[:, :, 1] * n_col + col]
-    )
-    own_places = lax.dynamic_index_in_dim(all_x, col, 3, keepdims=False)[:, :, 0]
-    col_x = jnp.where(own_places >= 0, col_x, -1.0).reshape(2, -1)
-
-    row_z_padded = jnp.pad(row_z, ((0, 0), (0, ZSTEP - ZROWS)), constant_values=-1)
+    labelled = jnp.concatenate([tiles, meta])
+    own_tiles = send_all(labelled, "row", n_row // CORES, axis_index_groups=core_groups)
+    other_tiles = lax.ppermute(own_tiles, "row", [(n, n ^ 1) for n in range(n_row)])
+    core = row % CORES
+    devices = jnp.arange(n_col, dtype=jnp.float32)[:, None]
+    rows = jnp.arange(n_row // CORES) * CORES
+    rows = jnp.stack([rows + core, rows + 1 - core]).astype(jnp.float32)[:, :, None]
+    n_lines = 2 * n_col * XROWS // LANES
+
+    def listed_there(t):
+        found = t[:, -META : n_lines - META].astype(jnp.float32)
+        return found.reshape(n_row // CORES, 2, n_col, XROWS).transpose(1, 0, 2, 3)
+
+    def in_own_col(found, rows):
+        found = lax.dynamic_index_in_dim(found, col, 2, keepdims=False)
+        return numbers(found, n_row, rows, n_col, col).reshape(2, -1)
+
+    all_x = [listed_there(t) for t in (own_tiles, other_tiles)]
+    col_x = [in_own_col(found, rows[n]) for n, found in enumerate(all_x)]
+    all_x = jnp.stack(all_x, axis=1)
 
     def table(rows):
         return jax.ShapeDtypeStruct((rows, LANES), jnp.int32)
 
-    row_codes = decode(row_x)
-    square_list, cube_list = call(
-        match_kernel,
-        (),
-        (
-            sublanes(decode(z_codes)),
-            sublanes(decode(x_codes)),
-            row_codes,
-            decode(row_z_padded.reshape(-1)),
-            col_x,
-        ),
-        (table(ZROWS), table(XROWS)),
-    )
+    own_z = sublanes(own_z.astype(jnp.float32))
+    square_list = call(square_match, (), (own_z, row_x, *col_x), table(ZROWS))
 
     start = far_own * NEAR % n_row // CORES
-    cross = lax.dynamic_slice_in_dim(all_x, start, NEAR // CORES, 1)
-    rows = lax.dynamic_slice_in_dim(device, start, NEAR // CORES, 1)
+    cross = lax.dynamic_slice_in_dim(all_x, start, NEAR // CORES, 2)
+    rows = lax.dynamic_slice_in_dim(rows, start, NEAR // CORES, 1)
     in_order = core == 0
-    cross = jnp.where(in_order, cross, cross[::-1]).transpose(1, 0, 2, 3, 4)
-    rows = jnp.where(in_order, rows, rows[::-1]).transpose(1, 0).reshape(NEAR, 1, 1)
-    cross = cross.reshape(NEAR, 2, n_col, XROWS)
-    device = jnp.arange(n_col)[:, None]
-    cross_k = cross[:, 0] * n_row + rows
-    cross_j = cross[:, 1] * n_col + device.astype(jnp.float32)
-    cross_k = jnp.where((cross[:, 0] >= 0) & (device % NEAR == near_own), cross_k, -1.0)
-    cross_y = jnp.broadcast_to((device // NEAR).astype(jnp.float32), cross_j.shape)
-    cross_x = jnp.stack([cross_k, cross_j, cross_y], axis=1).reshape(NEAR, 3, -1)
-    near_z = lax.dynamic_slice_in_dim(row_z, far_own * NEAR, NEAR, 0).reshape(-1)
+    cross = jnp.where(in_order, cross, cross[:, ::-1]).transpose(0, 2, 1, 3, 4)
+    rows = jnp.where(in_order, rows, rows[::-1]).transpose(1, 0, 2).reshape(NEAR, 1, 1)
+    cross = cross.reshape(2, NEAR, n_col, XROWS)
+    cross = numbers(cross, n_row, rows, n_col, devices)
+    targets = jnp.arange(n_col)[:, None]
+    cross_k = jnp.where(targets % NEAR == near_own, cross[0], -1.0)
+    cross_y = jnp.broadcast_to((targets // NEAR).astype(jnp.float32), cross_k.shape)
+    cross_x = jnp.stack([cross_k, cross[1], cross_y], axis=1).reshape(NEAR, 3, -1)
+    near_z = lax.dynamic_slice_in_dim(row_z, far_own * NEAR, NEAR, 1).reshape(2, -1)
+    row_z = jnp.pad(row_z, ((0, 0), (0, 0), (0, ZSTEP - ZROWS)), constant_values=-1)
+    own_x = sublanes(own_x.astype(jnp.float32))
+    near_list, far_list = call(
+        cube_match,
+        (far_own.reshape(1),),
+        (own_x, row_z.reshape(2, -1), *col_x),
+        (table(XROWS), table(XROWS)),
+    )
     send_list, loads = call(
         send_kernel,
         (),
-        (sublanes(decode(near_z)), row_codes, cross_x),
-        (table(NEAR * ZROWS), table(1)),
+        (sublanes(near_z), row_x, cross_x),
+        (jax.ShapeDtypeStruct((n_far, SEGMENT), jnp.int32), table(1)),
+        [pltpu.VMEM((SEGMENT, LANES), jnp.float32)],
     )
     square = call(
         square_kernel,
         (square_list,),
-        (row_tiles, col_tiles),
+        (row_tiles, own_tiles, other_tiles),
         jax.ShapeDtypeStruct((NEAR, z_rows.shape[0] // 2, size, LANES), jnp.bfloat16),
-        sums_scratch(ZROWS),
+        [
+            *sums_scratch(ZROWS),
+            pltpu.VMEM(row_tiles.shape, row_tiles.dtype),
+            pltpu.SemaphoreType.DMA,
+        ],
+        far_off=1,
     )
     near = lax.all_to_all(
         square, "col", split_axis=0, concat_axis=0, axis_index_groups=near_groups
@@ -437,9 +483,9 @@
             packed, "col", split_axis=0, concat_axis=0, axis_index_groups=far_groups
         )
         return call(
-            cube_kernel,
-            (info, cube_list),
-            (near, far, col_tiles, base),
+            far_kernel,
+            (info, far_list),
+            (far, own_tiles, other_tiles, base),
             (
                 jax.ShapeDtypeStruct(base.shape, jnp.float32),
                 jax.ShapeDtypeStruct((1,), jnp.int32),
@@ -453,6 +499,13 @@
 
     used = jnp.repeat((x_rows >= 0).astype(jnp.float32), size)
     base = 1.5 * own.astype(jnp.float32) * used[None]
+    base = call(
+        near_kernel,
+        (near_list,),
+        (near, own_tiles, other_tiles, base),
+        jax.ShapeDtypeStruct(base.shape, jnp.float32),
+        sums_scratch(XROWS),
+    )
     state = (jnp.int32(2 * FIRST), *one_round(jnp.int32(0), base, FIRST))
     _, result, _ = lax.while_loop(lambda state: state[0] < state[2][0], next_round, state)
     return result[None, None]

time: 171 us -> 178 us (1.041)
  the two profiles are of different devices: /device:TPU:1 before, /device:TPU:259 now
where the time goes in v2:
time: 178 us; the launch traced here: 177 us
  waiting for transfers between devices  72.6 us (41%)
  Pallas kernels  29.7 us (17%)
  blocking collectives  26.8 us (15%)
  starting transfers between devices  25.7 us (14%)
  between operations  13.8 us (8%)
  local copies, waits for them, and re-layouts  6.61 us (4%)
    all_to_all x2, waiting for transfers between devices, one_round(): lax.all_to_all(packed, 'col', split_axis=0, concat_axis=0, axis_index_gro...  44.3 us
    pallas_call x9, Pallas kernels, call(): pl.pallas_call(kernel, out_shape=out, in_specs=[SMEM] * len(scalars) + [p...  29.7 us
    all_to_all x2, blocking collectives, send_all(): return lax.all_to_all(copies, axis, split_axis=0, concat_axis=0, **groups)  26.8 us
    all_to_all x1, waiting for transfers between devices, send_all(): return lax.all_to_all(copies, axis, split_axis=0, concat_axis=0, **groups)  18.1 us
    all_to_all x2, starting transfers between devices, one_round(): lax.all_to_all(packed, 'col', split_axis=0, concat_axis=0, axis_index_gro...  9.58 us
    all_to_all x1, waiting for transfers between devices, per_device(): lax.all_to_all(square, 'col', split_axis=0, concat_axis=0, axis_index_gro...  7.4 us
    all_to_all x1, starting transfers between devices, send_all(): return lax.all_to_all(copies, axis, split_axis=0, concat_axis=0, **groups)  6.68 us
    ppermute x1, starting transfers between devices, per_device(): lax.ppermute(own_tiles, 'row', [(n, n ^ 1) for n in range(n_row)])  5.16 us
  transfers between devices with their start and end apart: 6, of which 6 were waited for; matrix products, arithmetic and copies ran while one was open for 3% of the time, Pallas kernels for 6%

profile of v2, /device:TPU:259, one launch (start us, length us, event | category | flops | bytes accessed | tf_op | source)
XLA Modules:
  0.0 177.2 jit_solution(1749432041296475269)
XLA Ops:
  6.6 1.1 reshape_squeeze.3
  7.7 10.6 %all_to_all.31 = bf16[4,448,128]{2,1,0:T(8,128)(2,1)} all-to-all(bf16[4,448,128]{2,1,0:T(8,128)(2,1)S(1)} %broadcast_in_dim.89), channel_id=1, replica_groups={{0,1,2,3},{4,5,6,7},{8,9,10,11},{12,13,14,15},{16,17,18,19},{20,21,22,2..., dimensions={0} | all-to-all | bytes 917504 | tf_op jit(solution)/shard_map/all_to_all | solution.py:368
  18.5 16.2 %all_to_all.32 = s32[32,1,128]{2,1,0:T(1,128)S(1)} all-to-all(s32[32,1,128]{2,1,0:T(1,128)S(1)} %broadcast_in_dim.90), channel_id=1, replica_groups=mesh['row'=16,'col'=32] {'col'}, dimensions={0} | all-to-all | bytes 32768 | tf_op jit(solution)/shard_map/all_to_all | solution.py:368
  34.9 1.1 broadcast_in_dim.93
  36.0 6.7 %all-to-all-start.3 = ((bf16[8,464,128]{2,1,0:T(8,128)(2,1)}), bf16[8,464,128]{2,1,0:T(8,128)(2,1)S(1)}, u32[]{:S(2)}, u32[]{:S(2)}) async-start(bf16[8,464,128]{2,1,0:T(8,128)(2,1)} %broadcast_in_dim.93), calls=%async_computation.3 | async-start | bytes 1900544 | tf_op jit(solution)/shard_map/all_to_all | solution.py:368
  43.8 18.1 %all-to-all-done.3.own_tiles = bf16[8,464,128]{2,1,0:T(8,128)(2,1)S(1)} async-done(((bf16[8,464,128]{2,1,0:T(8,128)(2,1)}), bf16[8,464,128]{2,1,0:T(8,128)(2,1)S(1)}, u32[]{:S(2)}, u32[]{:S(2)}) %all-to-all-start.3) | async-done | bytes 950304 | tf_op jit(solution)/shard_map/all_to_all | solution.py:368
  61.9 5.2 %collective-permute-start = (bf16[8,464,128]{2,1,0:T(8,128)(2,1)S(1)}, bf16[8,464,128]{2,1,0:T(8,128)(2,1)S(1)}, u32[]{:S(2)}, u32[]{:S(2)}) collective-permute-start(bf16[8,464,128]{2,1,0:T(8,128)(2,1)S(1)} %all-to-all-done.3.own_tiles), channel_id=1, source_target_pairs={{0,32},{32,0},{64,96},{96,64},{128,160},{160,128},{192,224},{224,1... | collective-permute-start | bytes 2850824 | tf_op jit(solution)/shard_map/ppermute | solution.py:405
  67.3 0.1 reshape.544
  67.5 0.1 copy.48
  67.7 1.4 collective-permute-done.other_tiles
  69.2 0.1 reshape.546
  69.3 0.1 copy.49
  70.1 0.8 shard_map.57.lists
  71.0 0.6 copy-done
  71.7 1.3 all-gather.3.cloned.1.call-done.row_hbm
  73.0 6.2 %shard_map.58 = bf16[4,18,64,128]{3,2,1,0:T(8,128)(2,1)} custom-call(s32[40,128]{1,0:T(8,128)} %copy-done, bf16[32,448,128]{2,1,0:T(8,128)(2,1)} %all-gather.3.cloned.1.call-done.row_hbm, bf16[8,464,128]{2,1,0:T(8,128)(2,1)S(1)} %all-to-all-done.3.own_tiles, bf16[8,464,128]{2,1,0:T(8,128)(2,1)S(1)} %collective-permute-done.other_tiles), custom_call_target="tpu_custom_call" | custom-call | tf_op jit(solution)/shard_map/pallas_call | solution.py:333
  79.2 4.3 %all-to-all-start.4 = ((bf16[4,18,64,128]{3,2,1,0:T(8,128)(2,1)}), bf16[4,18,64,128]{3,2,1,0:T(8,128)(2,1)S(1)}, u32[]{:S(2)}, u32[]{:S(2)}) async-start(bf16[4,18,64,128]{3,2,1,0:T(8,128)(2,1)} %shard_map.58), calls=%async_computation.4 | async-start | bytes 2359296 | tf_op jit(solution)/shard_map/all_to_all | solution.py:470
  83.8 0.1 squeeze.11
  84.1 6.4 %shard_map.56 = (s32[8,256]{1,0:T(8,128)S(1)}, s32[1,128]{1,0:T(1,128)S(1)}) custom-call(f32[2,160,128]{2,1,0:T(8,128)S(1)} %broadcast_in_dim.98.near_z, f32[2,512]{1,0:T(2,128)S(1)} %convert_element_type.46.row_x, f32[4,3,512]{2,1,0:T(4,128)S(1)} %pad_maximum_fusion.cross_x), custom_call_target="tpu_custom_call" | custom-call | tf_op jit(solution)/shard_map/pallas_call | solution.py:333
  90.5 7.4 %all-to-all-done.4.near = bf16[4,18,64,128]{3,2,1,0:T(8,128)(2,1)S(1)} async-done(((bf16[4,18,64,128]{3,2,1,0:T(8,128)(2,1)}), bf16[4,18,64,128]{3,2,1,0:T(8,128)(2,1)S(1)}, u32[]{:S(2)}, u32[]{:S(2)}) %all-to-all-start.4) | async-done | bytes 1179680 | tf_op jit(solution)/shard_map/all_to_all | solution.py:470
  97.9 3.3 %shard_map.59 = bf16[8,784,128]{2,1,0:T(8,128)(2,1)} custom-call(s32[2]{0:T(128)S(1)} %pad_add_fusion.5.info, s32[1,128]{1,0:T(1,128)S(1)} %get-tuple-element.186.loads, s32[8,256]{1,0:T(8,128)S(1)} %get-tuple-element.187.lists, bf16[4,18,64,128]{3,2,1,0:T(8,128)(2,1)S(1)} %all-to-all-done.4.near), custom_call_target="tpu_custom_call" | custom-call | tf_op jit(solution)/shard_map/pallas_call | solution.py:333
  101.2 4.5 %all-to-all-start.5 = ((bf16[8,784,128]{2,1,0:T(8,128)(2,1)}), bf16[8,784,128]{2,1,0:T(8,128)(2,1)S(1)}, u32[]{:S(2)}, u32[]{:S(2)}) async-start(bf16[8,784,128]{2,1,0:T(8,128)(2,1)} %shard_map.59), calls=%async_computation.5 | async-start | bytes 3211264 | tf_op jit(solution)/shard_map/all_to_all | solution.py:482
  106.0 1.4 shard_map.55
  107.4 2.5 %shard_map.60.base = f32[64,896]{1,0:T(8,128)S(1)} custom-call(s32[16,128]{1,0:T(8,128)S(1)} %get-tuple-element.70.lists, bf16[4,18,64,128]{3,2,1,0:T(8,128)(2,1)} %copy-done.1, bf16[8,464,128]{2,1,0:T(8,128)(2,1)S(1)} %all-to-all-done.3.own_tiles, bf16[8,464,128]{2,1,0:T(8,128)(2,1)} %copy-done.2, f32[64,896]{1,0:T(8,128)S(1)} %convert_multiply_fusion.base), custom_call_target="tpu_custom_call" | custom-call | tf_op jit(solution)/shard_map/pallas_call | solution.py:333
  109.9 34.7 %all-to-all-done.5.far = bf16[8,784,128]{2,1,0:T(8,128)(2,1)S(1)} async-done(((bf16[8,784,128]{2,1,0:T(8,128)(2,1)}), bf16[8,784,128]{2,1,0:T(8,128)(2,1)S(1)}, u32[]{:S(2)}, u32[]{:S(2)}) %all-to-all-start.5) | async-done | bytes 1605664 | tf_op jit(solution)/shard_map/all_to_all | solution.py:482
  144.5 3.7 %shard_map.61 = (f32[64,896]{1,0:T(8,128)S(1)}, s32[1]{0:T(128)}) custom-call(s32[2]{0:T(128)S(1)} %pad_add_fusion.5.info, s32[16,128]{1,0:T(8,128)S(1)} %get-tuple-element.189.lists, bf16[8,784,128]{2,1,0:T(8,128)(2,1)S(1)} %all-to-all-done.5.far, bf16[8,464,128]{2,1,0:T(8,128)(2,1)S(1)} %all-to-all-done.3.own_tiles, bf16[8,464,128]{2,1,0:T(8,128)(2,1)} %copy-done.2, ...), custom_call_target="tpu_custom_call" | custom-call | tf_op jit(solution)/shard_map/pallas_call | solution.py:333
  148.2 21.4 %while.12 = (s32[]{:T(128)}, f32[64,896]{1,0:T(8,128)S(1)}, s32[1]{0:T(128)}, s32[]{:T(128)}, s32[1,128]{1,0:T(1,128)S(1)}, /*index=5*/s32[8,256]{1,0:T(8,128)S(...) while((s32[]{:T(128)}, f32[64,896]{1,0:T(8,128)S(1)}, ...), condition=%wide.region_1.2_spmd, body=%wide.region_0.1_spmd.sunk | while | flops 4 | bytes 5144761 | solution.py:510
  148.9 2.3 %body.2 = bf16[8,144,128]{2,1,0:T(8,128)(2,1)} custom-call(s32[2]{0:T(128)S(1)} %pad_add_fusion.7.info, s32[1,128]{1,0:T(1,128)S(1)} %get-tuple-element.208.loads, s32[8,256]{1,0:T(8,128)S(1)} %get-tuple-element.209.lists, bf16[4,18,64,128]{3,2,1,0:T(8,128)(2,1)} %get-tuple-element.210.near), custom_call_target="tpu_custom_call" | custom-call | tf_op jit(solution)/shard_map/while/body/pallas_call | solution.py:333
  151.2 5.1 %all-to-all-start = ((bf16[8,144,128]{2,1,0:T(8,128)(2,1)}), bf16[8,144,128]{2,1,0:T(8,128)(2,1)S(1)}, u32[]{:S(2)}, u32[]{:S(2)}) async-start(bf16[8,144,128]{2,1,0:T(8,128)(2,1)} %body.2), calls=%async_computation | async-start | bytes 589824 | tf_op jit(solution)/shard_map/while/body/all_to_all | solution.py:482
  156.3 9.7 %all-to-all-done.far = bf16[8,144,128]{2,1,0:T(8,128)(2,1)S(1)} async-done(((bf16[8,144,128]{2,1,0:T(8,128)(2,1)}), bf16[8,144,128]{2,1,0:T(8,128)(2,1)S(1)}, u32[]{:S(2)}, u32[]{:S(2)}) %all-to-all-start) | async-done | bytes 294944 | tf_op jit(solution)/shard_map/while/body/all_to_all | solution.py:482
  165.9 3.1 %body.3 = (f32[64,896]{1,0:T(8,128)S(1)}, s32[1]{0:T(128)}) custom-call(s32[2]{0:T(128)S(1)} %pad_add_fusion.7.info, s32[16,128]{1,0:T(8,128)S(1)} %get-tuple-element.211.lists, bf16[8,144,128]{2,1,0:T(8,128)(2,1)S(1)} %all-to-all-done.far, bf16[8,464,128]{2,1,0:T(8,128)(2,1)S(1)} %get-tuple-element.212.own_tiles, bf16[8,464,128]{2,1,0:T(8,128)(2,1)S(1)} %copy-done.3, ...), custom_call_target="tpu_custom_call" | custom-call | tf_op jit(solution)/shard_map/while/body/pallas_call | solution.py:333
  169.7 0.7 copy-done.4
  (102 shorter events, 3.5 us)
Async XLA Ops:
  6.5 11.8 %copy-start.6 = (s32[1,1,14]{2,1,0:T(1,128)S(1)}, s32[1,1,14]{2,1,0:T(1,128)}, u32[]{:S(2)}) copy-start(s32[1,1,14]{2,1,0:T(1,128)} %param.9) | copy-start | bytes 172
  6.5 11.8 %copy-start.9 = (s32[1,1,14]{2,1,0:T(1,128)S(1)}, s32[1,1,14]{2,1,0:T(1,128)}, u32[]{:S(2)}) copy-start(s32[1,1,14]{2,1,0:T(1,128)} %param.8) | copy-start | bytes 172
  6.5 11.8 %copy-start.7 = (s32[1,1,36]{2,1,0:T(1,128)S(1)}, s32[1,1,36]{2,1,0:T(1,128)}, u32[]{:S(2)}) copy-start(s32[1,1,36]{2,1,0:T(1,128)} %param.11) | copy-start | bytes 436
  6.5 11.8 %copy-start.8 = (s32[1,1,36]{2,1,0:T(1,128)S(1)}, s32[1,1,36]{2,1,0:T(1,128)}, u32[]{:S(2)}) copy-start(s32[1,1,36]{2,1,0:T(1,128)} %param.10) | copy-start | bytes 436
  6.5 66.4 %all-gather.3.cloned.1.call-start = ((), (), s32[]{:S(2)}) async-start(), calls=%async_computation.6 | async-start | bytes 4128768 | tf_op jit(solution)/shard_map/all_gather | solution.py:387
  36.0 25.9 %all-to-all-start.3 = ((bf16[8,464,128]{2,1,0:T(8,128)(2,1)}), bf16[8,464,128]{2,1,0:T(8,128)(2,1)S(1)}, u32[]{:S(2)}, u32[]{:S(2)}) async-start(bf16[8,464,128]{2,1,0:T(8,128)(2,1)} %broadcast_in_dim.93), calls=%async_computation.3 | async-start | bytes 1900544 | tf_op jit(solution)/shard_map/all_to_all | solution.py:368
  61.9 7.3 %collective-permute-start = (bf16[8,464,128]{2,1,0:T(8,128)(2,1)S(1)}, bf16[8,464,128]{2,1,0:T(8,128)(2,1)S(1)}, u32[]{:S(2)}, u32[]{:S(2)}) collective-permute-start(bf16[8,464,128]{2,1,0:T(8,128)(2,1)S(1)} %all-to-all-done.3.own_tiles), channel_id=1, source_target_pairs={{0,32},{32,0},{64,96},{96,64},{128,160},{160,128},{192,224},{224,1... | collective-permute-start | bytes 2850824 | tf_op jit(solution)/shard_map/ppermute | solution.py:405
  69.2 10.0 %copy-start.2 = (bf16[8,464,128]{2,1,0:T(8,128)(2,1)}, bf16[8,464,128]{2,1,0:T(8,128)(2,1)S(1)}, u32[]{:S(2)}) copy-start(bf16[8,464,128]{2,1,0:T(8,128)(2,1)S(1)} %collective-permute-done.other_tiles) | copy-start | bytes 2850820
  70.9 0.6 copy-start
  79.2 18.7 %all-to-all-start.4 = ((bf16[4,18,64,128]{3,2,1,0:T(8,128)(2,1)}), bf16[4,18,64,128]{3,2,1,0:T(8,128)(2,1)S(1)}, u32[]{:S(2)}, u32[]{:S(2)}) async-start(bf16[4,18,64,128]{3,2,1,0:T(8,128)(2,1)} %shard_map.58), calls=%async_computation.4 | async-start | bytes 2359296 | tf_op jit(solution)/shard_map/all_to_all | solution.py:470
  97.9 3.3 %copy-start.1 = (bf16[4,18,64,128]{3,2,1,0:T(8,128)(2,1)}, bf16[4,18,64,128]{3,2,1,0:T(8,128)(2,1)S(1)}, u32[]{:S(2)}) copy-start(bf16[4,18,64,128]{3,2,1,0:T(8,128)(2,1)S(1)} %all-to-all-done.4.near) | copy-start | bytes 3538948
  101.2 4.6 %copy-start.5 = (bf16[1,1,64,896]{3,2,1,0:T(8,128)(2,1)S(1)}, bf16[1,1,64,896]{3,2,1,0:T(8,128)(2,1)}, u32[]{:S(2)}) copy-start(bf16[1,1,64,896]{3,2,1,0:T(8,128)(2,1)} %param.7) | copy-start | bytes 344068
  101.2 43.4 %all-to-all-start.5 = ((bf16[8,784,128]{2,1,0:T(8,128)(2,1)}), bf16[8,784,128]{2,1,0:T(8,128)(2,1)S(1)}, u32[]{:S(2)}, u32[]{:S(2)}) async-start(bf16[8,784,128]{2,1,0:T(8,128)(2,1)} %shard_map.59), calls=%async_computation.5 | async-start | bytes 3211264 | tf_op jit(solution)/shard_map/all_to_all | solution.py:482
  148.8 17.1 %copy-start.3 = (bf16[8,464,128]{2,1,0:T(8,128)(2,1)S(1)}, bf16[8,464,128]{2,1,0:T(8,128)(2,1)}, u32[]{:S(2)}) copy-start(bf16[8,464,128]{2,1,0:T(8,128)(2,1)} %get-tuple-element.213.other_tiles) | copy-start | bytes 2850820 | tf_op jit(solution)/shard_map/while
  151.2 14.8 %all-to-all-start = ((bf16[8,144,128]{2,1,0:T(8,128)(2,1)}), bf16[8,144,128]{2,1,0:T(8,128)(2,1)S(1)}, u32[]{:S(2)}, u32[]{:S(2)}) async-start(bf16[8,144,128]{2,1,0:T(8,128)(2,1)} %body.2), calls=%async_computation | async-start | bytes 589824 | tf_op jit(solution)/shard_map/while/body/all_to_all | solution.py:482
  169.6 0.7 copy-start.4
Sparse Core Ops, SparseCore 0:
  18.5 54.4 all-gather.2

commit v3 on v2

--- a/solution.py
+++ b/solution.py
@@ -33,6 +33,10 @@
     return lax.broadcasted_iota(jnp.int32, (1, width), 1).astype(jnp.float32)
 
 
+def upright(row):
+    return jnp.broadcast_to(row, (LANES, LANES)).T
+
+
 def beside(*refs):
     return (jnp.concatenate([ref[n : n + 1, :] for ref in refs], axis=1) for n in range(2))
 
@@ -49,13 +53,13 @@
     return jnp.where((lane_numbers(LANES) == base + count) & good, value, table)
 
 
-def square_match(own_z, row_x, own_col, other_col, square_list):
+def square_match(own_z, row_x, own_col, other_col):
     row_i, row_m = row_x[0:1, :], row_x[1:2, :]
     col_m, col_k = beside(own_col, other_col)
     row_lanes, col_lanes = lane_numbers(row_i.shape[1]), lane_numbers(col_m.shape[1])
     lane = lane_numbers(LANES)
 
-    i, k = own_z[0][:, :1], own_z[1][:, :1]
+    i, k = (upright(own_z[n : n + 1, :])[:ZROWS, :1] for n in range(2))
     in_row, in_col = (row_i == i) & (i >= 0), (col_k == k) & (k >= 0)
     table = jnp.zeros((ZROWS, LANES), jnp.float32)
     count = jnp.zeros((ZROWS, 1), jnp.float32)
@@ -68,7 +72,7 @@
         table = put(table, 0, count, good, last)
         table = put(table, 8, count, good, found - 1)
         count = count + jnp.where(good, 1.0, 0.0)
-    square_list[...] = jnp.where(lane == COUNT, count, table).astype(jnp.int32)
+    return jnp.where(lane == COUNT, count, table).astype(jnp.int32)
 
 def cube_match(here, own_x, row_z, own_col, other_col, near_list, far_list):
     col_m, col_k = beside(own_col, other_col)
@@ -179,9 +183,7 @@
     return jnp.where(lane < 64, even, odd)
 
 
-def add_products(lists, rows, load_left, load_right, sums, chunks, wait=None):
-    sums[...] = jnp.zeros_like(sums)
-
+def list_chunks(lists, rows, chunks):
     def per_row(n, length):
         def one(t, length):
             chunks[length] = (n << 3) + t * CHUNK
@@ -192,8 +194,11 @@
     length = lax.fori_loop(0, rows - 1, per_row, 0)
     for spare in range(GROUP):
         chunks[length + spare] = (rows - 1) << 3
-    if wait is not None:
-        wait()
+    return lax.div(length + GROUP - 1, GROUP)
+
+
+def add_products(lists, groups, load_left, load_right, sums, chunks):
+    sums[...] = jnp.zeros_like(sums)
 
     def per_group(group, carry):
         values = []
@@ -205,7 +210,7 @@
                 place = jnp.minimum(start + t, NEIGH - 1)
                 good = (start + t < lists[row, COUNT]).astype(jnp.int32)
                 left.append(load_left(lists[row, place], good))
-                tile = load_right(lists[row, 8 + place])
+                tile = load_right(row, place)
                 right += [tile, tile]
             left, right = jnp.concatenate(left, axis=1), jnp.concatenate(right, axis=0)
             values.append((row, jnp.dot(left, right, preferred_element_type=jnp.float32)))
@@ -213,7 +218,7 @@
             sums[row] += value
         return carry
 
-    lax.fori_loop(0, lax.div(length + GROUP - 1, GROUP), per_group, 0)
+    lax.fori_loop(0, groups, per_group, 0)
 
 
 def tile_of(entry, step):
@@ -225,8 +230,8 @@
     return ref.at[pl.ds(pl.multiple_of(tile * 64, 64), 64), :]
 
 
-def x_tile(own, other, entry):
-    device, tile, half = tile_of(entry, XROWS)
+def x_tile(lists, own, other, row, place):
+    device, tile, half = tile_of(lists[row, 8 + place], XROWS)
     shift = own.shape[0].bit_length() - 1
     core, device = device >> shift, device & (own.shape[0] - 1)
     tiles = (rows_of(ref.at[device], tile)[...] for ref in (own, other))
@@ -235,28 +240,51 @@
 
 
 def square_kernel(
-    lists, row_hbm, own_tiles, other_tiles, out_ref, sums, chunks, row_tiles, arrived
+    row_hbm, own_z, row_x, own_col, other_col, own_tiles, other_tiles, out_ref, *scratch
 ):
-    fetch = pltpu.make_async_copy(row_hbm, row_tiles, arrived)
-    fetch.start()
+    sums, chunks, row_tiles, arrived, table, lists, listed, squares, sent = scratch
+    parts = arrived.shape[0]
+    step = row_tiles.shape[0] // parts
+    fetches = [
+        pltpu.make_async_copy(
+            row_hbm.at[pl.ds(n * step, step)], row_tiles.at[pl.ds(n * step, step)], arrived.at[n]
+        )
+        for n in range(parts)
+    ]
+    for fetch in fetches:
+        fetch.start()
+    table[...] = square_match(own_z, row_x, own_col, other_col)
+    known = pltpu.make_async_copy(table, lists, listed)
+    known.start()
+    known.wait()
+    groups = list_chunks(lists, ZROWS, chunks)
+    for fetch in fetches:
+        fetch.wait()
 
     def load_left(entry, good):
         device, tile, half = tile_of(entry, XROWS)
         return rows_of(row_tiles.at[device], tile)[...] * half_mask(half, good)
 
-    load_right = functools.partial(x_tile, own_tiles, other_tiles)
-    add_products(lists, ZROWS, load_left, load_right, sums, chunks, fetch.wait)
+    load_right = functools.partial(x_tile, lists, own_tiles, other_tiles)
+    add_products(lists, groups, load_left, load_right, sums, chunks)
 
     def store(n, carry):
         square = pair_up(sums[2 * n], sums[2 * n + 1]).astype(jnp.bfloat16)
         for copy in range(out_ref.shape[0]):
-            out_ref[copy, n] = square
+            squares[n] = square
         return carry
 
-    lax.fori_loop(0, out_ref.shape[1], store, 0, unroll=2)
-
-
-def pack_kernel(info, loads, lists, near, out_ref):
+    lax.fori_loop(0, squares.shape[0], store, 0, unroll=2)
+    copies = [
+        pltpu.make_async_copy(squares, out_ref.at[n], sent.at[n]) for n in range(out_ref.shape[0])
+    ]
+    for copy in copies:
+        copy.start()
+    for copy in copies:
+        copy.wait()
+
+
+def pack_kernel(info, loads, lists, near, sent_ref, out_ref, sent):
     out_ref[...] = jnp.zeros_like(out_ref)
     first, own = info[0], info[1]
     places = (out_ref.shape[1] - META) // 32
@@ -284,9 +312,19 @@
                 rows_of(out_ref.at[target], step * STEP + n)[...] = tile
             return carry
 
-        return lax.fori_loop(0, lax.div(number + 2 * STEP - 1, 2 * STEP), per_step, carry)
+        lax.fori_loop(0, lax.div(number + 2 * STEP - 1, 2 * STEP), per_step, 0)
+        copy_out(target).start()
+        return carry
+
+    def copy_out(target):
+        return pltpu.make_async_copy(out_ref.at[target], sent_ref.at[target], sent.at[target])
+
+    def finish(target, carry):
+        copy_out(target).wait()
+        return carry
 
     lax.fori_loop(0, out_ref.shape[0], per_target, 0)
+    lax.fori_loop(0, out_ref.shape[0], finish, 0)
 
 
 def subtract_cubes(sums, base, out_ref):
@@ -295,40 +333,65 @@
         out_ref[:, here] = base[:, here] - 0.5 * pair_up(sums[2 * n], sums[2 * n + 1])
 
 
-def near_kernel(lists, near, own_tiles, other_tiles, base, out_ref, sums, chunks):
+def near_kernel(
+    lists, far, near, own_tiles, other_tiles, base, out_ref, rights, ahead, sums, chunks
+):
     def load_left(entry, good):
         device, tile, half = tile_of(entry, ZSTEP)
         return near[device, tile] * half_mask(half, good)
 
-    load_right = functools.partial(x_tile, own_tiles, other_tiles)
-    add_products(lists, XROWS, load_left, load_right, sums, chunks)
+    load_right = functools.partial(x_tile, lists, own_tiles, other_tiles)
+    add_products(lists, list_chunks(lists, XROWS, chunks), load_left, load_right, sums, chunks)
     subtract_cubes(sums, base, out_ref)
-
-
-def far_kernel(
+    ahead[ahead.shape[0] - 1] = list_chunks(far, XROWS, ahead)
+
+    def ready(row, carry):
+        for place in range(NEIGH):
+            rights[row, place] = x_tile(far, own_tiles, other_tiles, row, place)
+        return carry
+
+    lax.fori_loop(0, XROWS, ready, 0)
+
+
+def largest(far, most_ref):
+    places = (far.shape[1] - META) // 32
+    most = far[0, places * 32 :, :]
+    for n in range(1, far.shape[0]):
+        most = jnp.maximum(most, far[n, places * 32 :, :])
+    most_ref[0] = jnp.max(most.astype(jnp.float32)).astype(jnp.int32)
+
+
+def far_tile(far, first, code, good):
+    places = (far.shape[1] - META) // 32
+    shift = far.shape[0].bit_length() - 1
+    group, place = code & (far.shape[0] - 1), (code >> shift) - first
+    good = good * ((place >= 0) & (place < places)).astype(jnp.int32)
+    place = jnp.clip(place, 0, places - 1)
+    return rows_of(far.at[group], place >> 1)[...] * half_mask(place & 1, good)
+
+
+def first_kernel(lists, ahead, base_hbm, far, rights, out_ref, most_ref, sums, base, arrived):
+    fetch = pltpu.make_async_copy(base_hbm, base, arrived)
+    fetch.start()
+    largest(far, most_ref)
+    groups = ahead[ahead.shape[0] - 1]
+    load_left = functools.partial(far_tile, far, 0)
+    add_products(lists, groups, load_left, lambda row, place: rights[row, place], sums, ahead)
+    fetch.wait()
+    subtract_cubes(sums, base, out_ref)
+
+
+def more_kernel(
     info, lists, far, own_tiles, other_tiles, base, out_ref, most_ref, sums, chunks
 ):
-    first = info[0]
-    n_groups = far.shape[0]
-    shift = n_groups.bit_length() - 1
-    places = (far.shape[1] - META) // 32
-    most = far[0, places * 32 :, :]
-    for n in range(1, n_groups):
-        most = jnp.maximum(most, far[n, places * 32 :, :])
-    most_ref[0] = jnp.max(most.astype(jnp.float32)).astype(jnp.int32)
-
-    def load_left(code, good):
-        group, place = code & (n_groups - 1), (code >> shift) - first
-        good = good * ((place >= 0) & (place < places)).astype(jnp.int32)
-        place = jnp.clip(place, 0, places - 1)
-        return rows_of(far.at[group], place >> 1)[...] * half_mask(place & 1, good)
-
-    load_right = functools.partial(x_tile, own_tiles, other_tiles)
-    add_products(lists, XROWS, load_left, load_right, sums, chunks)
+    largest(far, most_ref)
+    load_left = functools.partial(far_tile, far, info[0])
+    load_right = functools.partial(x_tile, lists, own_tiles, other_tiles)
+    add_products(lists, list_chunks(lists, XROWS, chunks), load_left, load_right, sums, chunks)
     subtract_cubes(sums, base, out_ref)
 
 
-def call(kernel, scalars, arrays, out, scratch=(), far_off=0):
+def call(kernel, scalars, arrays, out, scratch=(), far_off=0, out_spec=VMEM):
     single = isinstance(out, jax.ShapeDtypeStruct)
     return pl.pallas_call(
         kernel,
@@ -336,9 +399,9 @@
         in_specs=[SMEM] * len(scalars)
         + [pl.BlockSpec(memory_space=pl.ANY)] * far_off
         + [VMEM] * (len(arrays) - far_off),
-        out_specs=VMEM if single else [SMEM if o.shape == (1,) else VMEM for o in out],
+        out_specs=out_spec if single else [SMEM if len(o.shape) == 1 else VMEM for o in out],
         scratch_shapes=scratch,
-        compiler_params=pltpu.CompilerParams(vmem_limit_bytes=(58 if far_off else 20) * MIB),
+        compiler_params=pltpu.CompilerParams(vmem_limit_bytes=20 * MIB),
     )(*scalars, *arrays)
 
 
@@ -402,6 +465,8 @@
     meta = jnp.pad(meta, ((0, META - meta.shape[0]), (0, 0)))
     labelled = jnp.concatenate([tiles, meta])
     own_tiles = send_all(labelled, "row", n_row // CORES, axis_index_groups=core_groups)
+    own_z = jnp.pad(own_z, ((0, 0), (0, LANES - ZROWS)), constant_values=-1).astype(jnp.float32)
+    own_tiles, row_x, own_z = lax.optimization_barrier((own_tiles, row_x, own_z))
     other_tiles = lax.ppermute(own_tiles, "row", [(n, n ^ 1) for n in range(n_row)])
     core = row % CORES
     devices = jnp.arange(n_col, dtype=jnp.float32)[:, None]
@@ -417,15 +482,16 @@
         found = lax.dynamic_index_in_dim(found, col, 2, keepdims=False)
         return numbers(found, n_row, rows, n_col, col).reshape(2, -1)
 
-    all_x = [listed_there(t) for t in (own_tiles, other_tiles)]
-    col_x = [in_own_col(found, rows[n]) for n, found in enumerate(all_x)]
-    all_x = jnp.stack(all_x, axis=1)
+    own_listed = listed_there(own_tiles)
+    own_col = in_own_col(own_listed, rows[0])
+    other_tiles, own_col = lax.optimization_barrier((other_tiles, own_col))
+    other_listed = listed_there(other_tiles)
+    col_x = (own_col, in_own_col(other_listed, rows[1]))
+    all_x = jnp.stack([own_listed, other_listed], axis=1)
 
     def table(rows):
         return jax.ShapeDtypeStruct((rows, LANES), jnp.int32)
 
-    own_z = sublanes(own_z.astype(jnp.float32))
-    square_list = call(square_match, (), (own_z, row_x, *col_x), table(ZROWS))
 
     start = far_own * NEAR % n_row // CORES
     cross = lax.dynamic_slice_in_dim(all_x, start, NEAR // CORES, 2)
@@ -457,57 +523,91 @@
     )
     square = call(
         square_kernel,
-        (square_list,),
-        (row_tiles, own_tiles, other_tiles),
+        (),
+        (
+            pltpu.with_memory_space_constraint(row_tiles, pltpu.HBM),
+            own_z,
+            row_x,
+            *col_x,
+            own_tiles,
+            other_tiles,
+        ),
         jax.ShapeDtypeStruct((NEAR, z_rows.shape[0] // 2, size, LANES), jnp.bfloat16),
         [
             *sums_scratch(ZROWS),
             pltpu.VMEM(row_tiles.shape, row_tiles.dtype),
+            pltpu.SemaphoreType.DMA((4,)),
+            pltpu.VMEM((ZROWS, LANES), jnp.int32),
+            pltpu.SMEM((ZROWS, LANES), jnp.int32),
             pltpu.SemaphoreType.DMA,
+            pltpu.VMEM((z_rows.shape[0] // 2, size, LANES), jnp.bfloat16),
+            pltpu.SemaphoreType.DMA((NEAR,)),
         ],
         far_off=1,
+        out_spec=pl.BlockSpec(memory_space=pl.ANY),
     )
     near = lax.all_to_all(
         square, "col", split_axis=0, concat_axis=0, axis_index_groups=near_groups
     )
 
-    def one_round(first, base, count):
+    def exchange(first, count):
         info = jnp.stack([first, far_own])
         packed = call(
             pack_kernel,
             (info, loads, send_list),
             (near,),
             jax.ShapeDtypeStruct((n_far, count * size + META, LANES), jnp.bfloat16),
+            [
+                pltpu.VMEM((n_far, count * size + META, LANES), jnp.bfloat16),
+                pltpu.SemaphoreType.DMA((n_far,)),
+            ],
+            out_spec=pl.BlockSpec(memory_space=pl.ANY),
         )
         far = lax.all_to_all(
             packed, "col", split_axis=0, concat_axis=0, axis_index_groups=far_groups
         )
-        return call(
-            far_kernel,
+        return info, far
+
+    used = jnp.repeat((x_rows >= 0).astype(jnp.float32), size)
+    base = 1.5 * own.astype(jnp.float32) * used[None]
+    ahead = jax.ShapeDtypeStruct((XROWS * 4 + 2 * GROUP,), jnp.int32)
+    result, most = jax.ShapeDtypeStruct(base.shape, jnp.float32), jax.ShapeDtypeStruct((1,), jnp.int32)
+    rights = pltpu.VMEM((XROWS, NEIGH, size, LANES), own.dtype)
+    base, rights, ahead = call(
+        near_kernel,
+        (near_list, far_list),
+        (near, own_tiles, other_tiles, base),
+        (result, rights, ahead),
+        sums_scratch(XROWS),
+    )
+    _, far = exchange(jnp.int32(0), FIRST)
+    state = call(
+        first_kernel,
+        (far_list, ahead),
+        (pltpu.with_memory_space_constraint(base, pltpu.HBM), far, rights),
+        (result, most),
+        [
+            sums_scratch(XROWS)[0],
+            pltpu.VMEM(base.shape, jnp.float32),
+            pltpu.SemaphoreType.DMA,
+        ],
+        far_off=1,
+    )
+
+    def more(state):
+        first, base, _ = state
+        info, far = exchange(first, MORE)
+        base, largest_need = call(
+            more_kernel,
             (info, far_list),
             (far, own_tiles, other_tiles, base),
-            (
-                jax.ShapeDtypeStruct(base.shape, jnp.float32),
-                jax.ShapeDtypeStruct((1,), jnp.int32),
-            ),
+            (result, most),
             sums_scratch(XROWS),
         )
-
-    def next_round(state):
-        first, base, _ = state
-        return (first + 2 * MORE, *one_round(first, base, MORE))
-
-    used = jnp.repeat((x_rows >= 0).astype(jnp.float32), size)
-    base = 1.5 * own.astype(jnp.float32) * used[None]
-    base = call(
-        near_kernel,
-        (near_list,),
-        (near, own_tiles, other_tiles, base),
-        jax.ShapeDtypeStruct(base.shape, jnp.float32),
-        sums_scratch(XROWS),
-    )
-    state = (jnp.int32(2 * FIRST), *one_round(jnp.int32(0), base, FIRST))
-    _, result, _ = lax.while_loop(lambda state: state[0] < state[2][0], next_round, state)
+        return first + 2 * MORE, base, largest_need
+
+    state = (jnp.int32(2 * FIRST), *state)
+    _, result, _ = lax.while_loop(lambda state: state[0] < state[2][0], more, state)
     return result[None, None]
 
 

time: 178 us -> 164 us (0.921)
  the two profiles are of different devices: /device:TPU:259 before, /device:TPU:1 now
where the time goes in v3:
time: 164 us; the launch traced here: 163 us
  waiting for transfers between devices  71 us (43%)
  starting transfers between devices  32.8 us (20%)
  Pallas kernels  23.8 us (15%)
  between operations  13.9 us (8%)
  blocking collectives  11.3 us (7%)
  local copies, waits for them, and re-layouts  8.07 us (5%)
    all_to_all x1, waiting for transfers between devices, exchange(): lax.all_to_all(packed, 'col', split_axis=0, concat_axis=0, axis_index_gro...  32.4 us
    all_to_all x2, waiting for transfers between devices, send_all(): return lax.all_to_all(copies, axis, split_axis=0, concat_axis=0, **groups)  30.8 us
    pallas_call x6, Pallas kernels, call(): pl.pallas_call(kernel, out_shape=out, in_specs=[SMEM] * len(scalars) + [p...  23.8 us
    all_to_all x2, starting transfers between devices, send_all(): return lax.all_to_all(copies, axis, split_axis=0, concat_axis=0, **groups)  18.8 us
    all_to_all x1, blocking collectives, send_all(): return lax.all_to_all(copies, axis, split_axis=0, concat_axis=0, **groups)  11.3 us
    all_to_all x1, waiting for transfers between devices, per_device(): lax.all_to_all(square, 'col', split_axis=0, concat_axis=0, axis_index_gro...  6.99 us
    ppermute x1, starting transfers between devices, per_device(): lax.ppermute(own_tiles, 'row', [(n, n ^ 1) for n in range(n_row)])  5.94 us
    all_to_all x1, starting transfers between devices, exchange(): lax.all_to_all(packed, 'col', split_axis=0, concat_axis=0, axis_index_gro...  4.48 us
  transfers between devices with their start and end apart: 6, of which 5 were waited for; matrix products, arithmetic and copies ran while one was open for 4% of the time, Pallas kernels for 8%

profile of v3, /device:TPU:1, one launch (start us, length us, event | category | flops | bytes accessed | tf_op | source)
XLA Modules:
  0.0 163.0 jit_solution(15169606397009663294)
XLA Ops:
  6.6 1.1 reshape_squeeze.3
  7.7 11.3 %all_to_all.31 = bf16[4,448,128]{2,1,0:T(8,128)(2,1)} all-to-all(bf16[4,448,128]{2,1,0:T(8,128)(2,1)S(1)} %broadcast_in_dim.83), channel_id=1, replica_groups={{0,1,2,3},{4,5,6,7},{8,9,10,11},{12,13,14,15},{16,17,18,19},{20,21,22,2..., dimensions={0} | all-to-all | bytes 917504 | tf_op jit(solution)/shard_map/all_to_all | solution.py:431
  19.3 0.6 broadcast_in_dim.84
  19.9 8.8 %all-to-all-start.2 = ((s32[32,1,128]{2,1,0:T(1,128)}), s32[32,1,128]{2,1,0:T(1,128)S(1)}, u32[]{:S(2)}, u32[]{:S(2)}) async-start(s32[32,1,128]{2,1,0:T(1,128)} %broadcast_in_dim.84), calls=%async_computation.2 | async-start | bytes 32768 | tf_op jit(solution)/shard_map/all_to_all | solution.py:431
  28.8 8.4 %all-to-all-done.2 = s32[32,1,128]{2,1,0:T(1,128)S(1)} async-done(((s32[32,1,128]{2,1,0:T(1,128)}), s32[32,1,128]{2,1,0:T(1,128)S(1)}, u32[]{:S(2)}, u32[]{:S(2)}) %all-to-all-start.2) | async-done | bytes 16416 | tf_op jit(solution)/shard_map/all_to_all | solution.py:431
  37.4 1.1 broadcast_in_dim.87
  38.5 10.0 %all-to-all-start.3 = ((bf16[8,464,128]{2,1,0:T(8,128)(2,1)}), bf16[8,464,128]{2,1,0:T(8,128)(2,1)S(1)}, u32[]{:S(2)}, u32[]{:S(2)}) async-start(bf16[8,464,128]{2,1,0:T(8,128)(2,1)} %broadcast_in_dim.87), calls=%async_computation.3 | async-start | bytes 1900544 | tf_op jit(solution)/shard_map/all_to_all | solution.py:431
  49.7 22.3 %all-to-all-done.3.own_tiles = bf16[8,464,128]{2,1,0:T(8,128)(2,1)S(1)} async-done(((bf16[8,464,128]{2,1,0:T(8,128)(2,1)}), bf16[8,464,128]{2,1,0:T(8,128)(2,1)S(1)}, u32[]{:S(2)}, u32[]{:S(2)}) %all-to-all-start.3) | async-done | bytes 950304 | tf_op jit(solution)/shard_map/all_to_all | solution.py:431
  72.1 5.9 %collective-permute-start = (bf16[8,464,128]{2,1,0:T(8,128)(2,1)S(1)}, bf16[8,464,128]{2,1,0:T(8,128)(2,1)S(1)}, u32[]{:S(2)}, u32[]{:S(2)}) collective-permute-start(bf16[8,464,128]{2,1,0:T(8,128)(2,1)S(1)} %all-to-all-done.3.own_tiles), channel_id=1, source_target_pairs={{0,32},{32,0},{64,96},{96,64},{128,160},{160,128},{192,224},{224,1... | collective-permute-start | bytes 2850824 | tf_op jit(solution)/shard_map/ppermute | solution.py:470
  78.1 0.6 copy-done.8
  78.8 0.1 reshape.546
  78.9 0.1 copy.47
  79.4 0.7 collective-permute-done.other_tiles
  80.2 0.1 reshape.548
  80.3 0.1 copy.48
  80.9 6.2 %shard_map.56 = bf16[4,18,64,128]{3,2,1,0:T(8,128)(2,1)} custom-call(bf16[32,448,128]{2,1,0:T(8,128)(2,1)} %all-gather.3.cloned.1.call-done.row_hbm, f32[2,128]{1,0:T(2,128)S(1)} %pad_convert_fusion.own_z, f32[2,512]{1,0:T(2,128)S(1)} %convert_element_type.45.row_x, f32[2,128]{1,0:T(2,128)S(1)} %maximum_select_fusion.1.own_col, ...), custom_call_target="tpu_custom_call" | custom-call | tf_op jit(solution)/shard_map/pallas_call | solution.py:396
  87.2 3.5 %all-to-all-start.4 = ((bf16[4,18,64,128]{3,2,1,0:T(8,128)(2,1)}), bf16[4,18,64,128]{3,2,1,0:T(8,128)(2,1)S(1)}, u32[]{:S(2)}, u32[]{:S(2)}) async-start(bf16[4,18,64,128]{3,2,1,0:T(8,128)(2,1)} %shard_map.56), calls=%async_computation.4 | async-start | bytes 2359296 | tf_op jit(solution)/shard_map/all_to_all | solution.py:549
  90.8 0.1 squeeze.11
  91.0 0.1 stack.78
  91.2 0.1 broadcast_in_dim.93.near_z
  91.3 6.4 %shard_map.58 = (s32[8,256]{1,0:T(8,128)S(1)}, s32[1,128]{1,0:T(1,128)S(1)}) custom-call(f32[2,160,128]{2,1,0:T(8,128)S(1)} %broadcast_in_dim.93.near_z, f32[2,512]{1,0:T(2,128)S(1)} %convert_element_type.45.row_x, f32[4,3,512]{2,1,0:T(4,128)S(1)} %pad_maximum_fusion.cross_x), custom_call_target="tpu_custom_call" | custom-call | tf_op jit(solution)/shard_map/pallas_call | solution.py:396
  97.7 7.0 %all-to-all-done.4.near = bf16[4,18,64,128]{3,2,1,0:T(8,128)(2,1)S(1)} async-done(((bf16[4,18,64,128]{3,2,1,0:T(8,128)(2,1)}), bf16[4,18,64,128]{3,2,1,0:T(8,128)(2,1)S(1)}, u32[]{:S(2)}, u32[]{:S(2)}) %all-to-all-start.4) | async-done | bytes 1179680 | tf_op jit(solution)/shard_map/all_to_all | solution.py:549
  104.7 2.6 %shard_map.59 = bf16[8,784,128]{2,1,0:T(8,128)(2,1)} custom-call(s32[2]{0:T(128)S(1)} %pad_add_fusion.5.info, s32[1,128]{1,0:T(1,128)S(1)} %get-tuple-element.198.loads, s32[8,256]{1,0:T(8,128)S(1)} %get-tuple-element.199.lists, bf16[4,18,64,128]{3,2,1,0:T(8,128)(2,1)S(1)} %all-to-all-done.4.near), custom_call_target="tpu_custom_call" | custom-call | tf_op jit(solution)/shard_map/pallas_call | solution.py:396
  107.4 4.5 %all-to-all-start.5 = ((bf16[8,784,128]{2,1,0:T(8,128)(2,1)}), bf16[8,784,128]{2,1,0:T(8,128)(2,1)S(1)}, u32[]{:S(2)}, u32[]{:S(2)}) async-start(bf16[8,784,128]{2,1,0:T(8,128)(2,1)} %shard_map.59), calls=%async_computation.5 | async-start | bytes 3211264 | tf_op jit(solution)/shard_map/all_to_all | solution.py:566
  112.0 0.7 convert_multiply_fusion.base
  112.9 1.4 shard_map.55
  114.3 0.9 copy-done
  115.3 4.6 %shard_map.57 = (f32[64,896]{1,0:T(8,128)S(1)}, bf16[16,7,64,128]{3,2,1,0:T(8,128)(2,1)S(1)}, s32[80]{0:T(128)S(1)}) custom-call(s32[16,128]{1,0:T(8,128)S(1)} %get-tuple-element.79.lists, s32[16,128]{1,0:T(8,128)S(1)} %get-tuple-element.201.far.lists, bf16[4,18,64,128]{3,2,1,0:T(8,128)(2,1)} %copy-done.2, bf16[8,464,128]{2,1,0:T(8,128)(2,1)} %copy-done.3, ...), custom_call_target="tpu_custom_call" | custom-call | tf_op jit(solution)/shard_map/pallas_call | solution.py:396
  119.9 0.7 copy-done.1
  120.6 32.4 %all-to-all-done.5.far = bf16[8,784,128]{2,1,0:T(8,128)(2,1)S(1)} async-done(((bf16[8,784,128]{2,1,0:T(8,128)(2,1)}), bf16[8,784,128]{2,1,0:T(8,128)(2,1)S(1)}, u32[]{:S(2)}, u32[]{:S(2)}) %all-to-all-start.5) | async-done | bytes 1605664 | tf_op jit(solution)/shard_map/all_to_all | solution.py:566
  153.0 2.5 %shard_map.60 = (f32[64,896]{1,0:T(8,128)}, s32[1]{0:T(128)}) custom-call(s32[16,128]{1,0:T(8,128)S(1)} %get-tuple-element.201.far.lists, s32[80]{0:T(128)S(1)} %get-tuple-element.82.ahead, f32[64,896]{1,0:T(8,128)} %copy-done.1, bf16[8,784,128]{2,1,0:T(8,128)(2,1)S(1)} %all-to-all-done.5.far, bf16[16,7,64,128]{3,2,1,0:T(8,128)(2,1)S(1)} %get-tuple-element.86.rights), custom_call_target="tpu_custom_call" | custom-call | tf_op jit(solution)/shard_map/pallas_call | solution.py:396
  155.5 0.6 while.12
  (101 shorter events, 3.2 us)
Async XLA Ops:
  6.5 12.6 %copy-start.11 = (s32[1,1,36]{2,1,0:T(1,128)S(1)}, s32[1,1,36]{2,1,0:T(1,128)}, u32[]{:S(2)}) copy-start(s32[1,1,36]{2,1,0:T(1,128)} %param.10) | copy-start | bytes 436
  6.5 12.6 %copy-start.10 = (s32[1,1,36]{2,1,0:T(1,128)S(1)}, s32[1,1,36]{2,1,0:T(1,128)}, u32[]{:S(2)}) copy-start(s32[1,1,36]{2,1,0:T(1,128)} %param.11) | copy-start | bytes 436
  6.5 12.6 %copy-start.13 = (s32[1,1,14]{2,1,0:T(1,128)S(1)}, s32[1,1,14]{2,1,0:T(1,128)}, u32[]{:S(2)}) copy-start(s32[1,1,14]{2,1,0:T(1,128)} %param.8) | copy-start | bytes 172
  6.5 12.6 %copy-start.12 = (s32[1,1,14]{2,1,0:T(1,128)S(1)}, s32[1,1,14]{2,1,0:T(1,128)}, u32[]{:S(2)}) copy-start(s32[1,1,14]{2,1,0:T(1,128)} %param.9) | copy-start | bytes 172
  6.5 74.4 %all-gather.3.cloned.1.call-start = ((), (), s32[]{:S(2)}) async-start(), calls=%async_computation.6 | async-start | bytes 4128768 | tf_op jit(solution)/shard_map/all_gather | solution.py:450
  19.9 17.3 %all-to-all-start.2 = ((s32[32,1,128]{2,1,0:T(1,128)}), s32[32,1,128]{2,1,0:T(1,128)S(1)}, u32[]{:S(2)}, u32[]{:S(2)}) async-start(s32[32,1,128]{2,1,0:T(1,128)} %broadcast_in_dim.84), calls=%async_computation.2 | async-start | bytes 32768 | tf_op jit(solution)/shard_map/all_to_all | solution.py:431
  38.5 33.6 %all-to-all-start.3 = ((bf16[8,464,128]{2,1,0:T(8,128)(2,1)}), bf16[8,464,128]{2,1,0:T(8,128)(2,1)S(1)}, u32[]{:S(2)}, u32[]{:S(2)}) async-start(bf16[8,464,128]{2,1,0:T(8,128)(2,1)} %broadcast_in_dim.87), calls=%async_computation.3 | async-start | bytes 1900544 | tf_op jit(solution)/shard_map/all_to_all | solution.py:431
  72.1 15.0 %copy-start.3 = (bf16[8,464,128]{2,1,0:T(8,128)(2,1)}, bf16[8,464,128]{2,1,0:T(8,128)(2,1)S(1)}, u32[]{:S(2)}) copy-start(bf16[8,464,128]{2,1,0:T(8,128)(2,1)S(1)} %all-to-all-done.3.own_tiles) | copy-start | bytes 2850820
  72.1 8.1 %collective-permute-start = (bf16[8,464,128]{2,1,0:T(8,128)(2,1)S(1)}, bf16[8,464,128]{2,1,0:T(8,128)(2,1)S(1)}, u32[]{:S(2)}, u32[]{:S(2)}) collective-permute-start(bf16[8,464,128]{2,1,0:T(8,128)(2,1)S(1)} %all-to-all-done.3.own_tiles), channel_id=1, source_target_pairs={{0,32},{32,0},{64,96},{96,64},{128,160},{160,128},{192,224},{224,1... | collective-permute-start | bytes 2850824 | tf_op jit(solution)/shard_map/ppermute | solution.py:470
  78.1 0.6 copy-start.8
  80.2 7.0 %copy-start.5 = (bf16[8,464,128]{2,1,0:T(8,128)(2,1)}, bf16[8,464,128]{2,1,0:T(8,128)(2,1)S(1)}, u32[]{:S(2)}) copy-start(bf16[8,464,128]{2,1,0:T(8,128)(2,1)S(1)} %collective-permute-done.other_tiles) | copy-start | bytes 2850820
  87.2 17.6 %all-to-all-start.4 = ((bf16[4,18,64,128]{3,2,1,0:T(8,128)(2,1)}), bf16[4,18,64,128]{3,2,1,0:T(8,128)(2,1)S(1)}, u32[]{:S(2)}, u32[]{:S(2)}) async-start(bf16[4,18,64,128]{3,2,1,0:T(8,128)(2,1)} %shard_map.56), calls=%async_computation.4 | async-start | bytes 2359296 | tf_op jit(solution)/shard_map/all_to_all | solution.py:549
  104.7 2.7 %copy-start.2 = (bf16[4,18,64,128]{3,2,1,0:T(8,128)(2,1)}, bf16[4,18,64,128]{3,2,1,0:T(8,128)(2,1)S(1)}, u32[]{:S(2)}) copy-start(bf16[4,18,64,128]{3,2,1,0:T(8,128)(2,1)S(1)} %all-to-all-done.4.near) | copy-start | bytes 3538948
  107.4 4.7 %copy-start.7 = (bf16[1,1,64,896]{3,2,1,0:T(8,128)(2,1)S(1)}, bf16[1,1,64,896]{3,2,1,0:T(8,128)(2,1)}, u32[]{:S(2)}) copy-start(bf16[1,1,64,896]{3,2,1,0:T(8,128)(2,1)} %param.7) | copy-start | bytes 344068
  107.4 5.4 %copy-start.9 = (f32[2,32,40]{2,1,0:T(8,128)S(1)}, f32[2,32,40]{2,1,0:T(8,128)}, u32[]{:S(2)}) copy-start(f32[2,32,40]{2,1,0:T(8,128)} %copy-done.8) | copy-start | bytes 30724
  107.4 45.6 %all-to-all-start.5 = ((bf16[8,784,128]{2,1,0:T(8,128)(2,1)}), bf16[8,784,128]{2,1,0:T(8,128)(2,1)S(1)}, u32[]{:S(2)}, u32[]{:S(2)}) async-start(bf16[8,784,128]{2,1,0:T(8,128)(2,1)} %shard_map.59), calls=%async_computation.5 | async-start | bytes 3211264 | tf_op jit(solution)/shard_map/all_to_all | solution.py:566
  114.3 0.9 copy-start
  119.9 0.7 copy-start.1
Sparse Core Ops, SparseCore 0:
  19.2 57.4 all-gather.2

commit v4 on v3

--- a/solution.py
+++ b/solution.py
@@ -20,7 +20,7 @@
 META = 16
 LANES = 128
 CHUNK = 2
-GROUP = 8
+GROUP = 16
 STEP = 2
 COUNT = 32
 FAR = 1e9
@@ -164,7 +164,8 @@
 
 def half_mask(half, good):
     lane = lax.broadcasted_iota(jnp.int32, (1, LANES), 1)
-    return jnp.where((lane >> 6 == half) & (good > 0), 1.0, 0.0).astype(jnp.bfloat16)
+    kept = jnp.where(good > 0, half, 2)
+    return jnp.where(lane >> 6 == kept, 1.0, 0.0).astype(jnp.bfloat16)
 
 
 def flat(value):
@@ -184,14 +185,11 @@
 
 
 def list_chunks(lists, rows, chunks):
-    def per_row(n, length):
-        def one(t, length):
-            chunks[length] = (n << 3) + t * CHUNK
-            return length + 1
-
-        return lax.fori_loop(0, lax.div(lists[n, COUNT] + CHUNK - 1, CHUNK), one, length)
-
-    length = lax.fori_loop(0, rows - 1, per_row, 0)
+    length = jnp.int32(0)
+    for n in range(rows - 1):
+        for start in range(0, NEIGH, CHUNK):
+            chunks[length + start // CHUNK] = (n << 3) + start
+        length = length + lax.div(lists[n, COUNT] + CHUNK - 1, CHUNK)
     for spare in range(GROUP):
         chunks[length + spare] = (rows - 1) << 3
     return lax.div(length + GROUP - 1, GROUP)
@@ -323,7 +321,8 @@
         copy_out(target).wait()
         return carry
 
-    lax.fori_loop(0, out_ref.shape[0], per_target, 0)
+    for target in range(out_ref.shape[0]):
+        per_target(target, 0)
     lax.fori_loop(0, out_ref.shape[0], finish, 0)
 
 

time: 164 us -> 164 us (level)
    all_to_all x1, waiting for transfers between devices: 32.4 us -> 30.4 us  [exchange(): lax.all_to_all(packed, 'col', split_axis=0, concat_axis=0, axis_index_gro...]
  transfers between devices with their start and end apart: 6 -> 6, of which waited for: 5 -> 5; matrix products, arithmetic and copies ran while one was open for 4% -> 4% of each run, Pallas kernels for 8% -> 7%
where the time goes in v4:
time: 164 us; the launch traced here: 162 us
  waiting for transfers between devices  69.8 us (43%)
  starting transfers between devices  32.7 us (20%)
  Pallas kernels  23.8 us (15%)
  between operations  13.9 us (8%)
  blocking collectives  11.3 us (7%)
  local copies, waits for them, and re-layouts  8.07 us (5%)
    all_to_all x2, waiting for transfers between devices, send_all(): return lax.all_to_all(copies, axis, split_axis=0, concat_axis=0, **groups)  30.8 us
    all_to_all x1, waiting for transfers between devices, exchange(): lax.all_to_all(packed, 'col', split_axis=0, concat_axis=0, axis_index_gro...  30.4 us
    pallas_call x6, Pallas kernels, call(): pl.pallas_call(kernel, out_shape=out, in_specs=[SMEM] * len(scalars) + [p...  23.8 us
    all_to_all x2, starting transfers between devices, send_all(): return lax.all_to_all(copies, axis, split_axis=0, concat_axis=0, **groups)  18.8 us
    all_to_all x1, blocking collectives, send_all(): return lax.all_to_all(copies, axis, split_axis=0, concat_axis=0, **groups)  11.3 us
    all_to_all x1, waiting for transfers between devices, per_device(): lax.all_to_all(square, 'col', split_axis=0, concat_axis=0, axis_index_gro...  7.85 us
    ppermute x1, starting transfers between devices, per_device(): lax.ppermute(own_tiles, 'row', [(n, n ^ 1) for n in range(n_row)])  5.94 us
    all_to_all x1, starting transfers between devices, per_device(): lax.all_to_all(square, 'col', split_axis=0, concat_axis=0, axis_index_gro...  4.19 us
  transfers between devices with their start and end apart: 6, of which 5 were waited for; matrix products, arithmetic and copies ran while one was open for 4% of the time, Pallas kernels for 7%

profile of v4, /device:TPU:1, one launch (start us, length us, event | category | flops | bytes accessed | tf_op | source)
XLA Modules:
  0.0 161.7 jit_solution(5396694189433743276)
XLA Ops:
  6.6 1.1 reshape_squeeze.3
  7.7 11.3 %all_to_all.31 = bf16[4,448,128]{2,1,0:T(8,128)(2,1)} all-to-all(bf16[4,448,128]{2,1,0:T(8,128)(2,1)S(1)} %broadcast_in_dim.83), channel_id=1, replica_groups={{0,1,2,3},{4,5,6,7},{8,9,10,11},{12,13,14,15},{16,17,18,19},{20,21,22,2..., dimensions={0} | all-to-all | bytes 917504 | tf_op jit(solution)/shard_map/all_to_all | solution.py:430
  19.3 0.6 broadcast_in_dim.84
  19.9 8.8 %all-to-all-start.2 = ((s32[32,1,128]{2,1,0:T(1,128)}), s32[32,1,128]{2,1,0:T(1,128)S(1)}, u32[]{:S(2)}, u32[]{:S(2)}) async-start(s32[32,1,128]{2,1,0:T(1,128)} %broadcast_in_dim.84), calls=%async_computation.2 | async-start | bytes 32768 | tf_op jit(solution)/shard_map/all_to_all | solution.py:430
  28.8 8.4 %all-to-all-done.2 = s32[32,1,128]{2,1,0:T(1,128)S(1)} async-done(((s32[32,1,128]{2,1,0:T(1,128)}), s32[32,1,128]{2,1,0:T(1,128)S(1)}, u32[]{:S(2)}, u32[]{:S(2)}) %all-to-all-start.2) | async-done | bytes 16416 | tf_op jit(solution)/shard_map/all_to_all | solution.py:430
  37.4 1.1 broadcast_in_dim.87
  38.5 10.0 %all-to-all-start.3 = ((bf16[8,464,128]{2,1,0:T(8,128)(2,1)}), bf16[8,464,128]{2,1,0:T(8,128)(2,1)S(1)}, u32[]{:S(2)}, u32[]{:S(2)}) async-start(bf16[8,464,128]{2,1,0:T(8,128)(2,1)} %broadcast_in_dim.87), calls=%async_computation.3 | async-start | bytes 1900544 | tf_op jit(solution)/shard_map/all_to_all | solution.py:430
  49.7 22.3 %all-to-all-done.3.own_tiles = bf16[8,464,128]{2,1,0:T(8,128)(2,1)S(1)} async-done(((bf16[8,464,128]{2,1,0:T(8,128)(2,1)}), bf16[8,464,128]{2,1,0:T(8,128)(2,1)S(1)}, u32[]{:S(2)}, u32[]{:S(2)}) %all-to-all-start.3) | async-done | bytes 950304 | tf_op jit(solution)/shard_map/all_to_all | solution.py:430
  72.1 5.9 %collective-permute-start = (bf16[8,464,128]{2,1,0:T(8,128)(2,1)S(1)}, bf16[8,464,128]{2,1,0:T(8,128)(2,1)S(1)}, u32[]{:S(2)}, u32[]{:S(2)}) collective-permute-start(bf16[8,464,128]{2,1,0:T(8,128)(2,1)S(1)} %all-to-all-done.3.own_tiles), channel_id=1, source_target_pairs={{0,32},{32,0},{64,96},{96,64},{128,160},{160,128},{192,224},{224,1... | collective-permute-start | bytes 2850824 | tf_op jit(solution)/shard_map/ppermute | solution.py:469
  78.1 0.6 copy-done.8
  78.8 0.1 reshape.546
  78.9 0.1 copy.47
  79.4 0.7 collective-permute-done.other_tiles
  80.2 0.1 reshape.548
  80.3 0.1 copy.48
  80.9 5.6 %shard_map.56 = bf16[4,18,64,128]{3,2,1,0:T(8,128)(2,1)} custom-call(bf16[32,448,128]{2,1,0:T(8,128)(2,1)} %all-gather.3.cloned.1.call-done.row_hbm, f32[2,128]{1,0:T(2,128)S(1)} %pad_convert_fusion.own_z, f32[2,512]{1,0:T(2,128)S(1)} %convert_element_type.45.row_x, f32[2,128]{1,0:T(2,128)S(1)} %maximum_select_fusion.1.own_col, ...), custom_call_target="tpu_custom_call" | custom-call | tf_op jit(solution)/shard_map/pallas_call | solution.py:395
  86.6 4.2 %all-to-all-start.4 = ((bf16[4,18,64,128]{3,2,1,0:T(8,128)(2,1)}), bf16[4,18,64,128]{3,2,1,0:T(8,128)(2,1)S(1)}, u32[]{:S(2)}, u32[]{:S(2)}) async-start(bf16[4,18,64,128]{3,2,1,0:T(8,128)(2,1)} %shard_map.56), calls=%async_computation.4 | async-start | bytes 2359296 | tf_op jit(solution)/shard_map/all_to_all | solution.py:548
  90.9 0.1 squeeze.11
  91.1 0.1 stack.78
  91.3 0.1 broadcast_in_dim.93.near_z
  91.4 6.4 %shard_map.58 = (s32[8,256]{1,0:T(8,128)S(1)}, s32[1,128]{1,0:T(1,128)S(1)}) custom-call(f32[2,160,128]{2,1,0:T(8,128)S(1)} %broadcast_in_dim.93.near_z, f32[2,512]{1,0:T(2,128)S(1)} %convert_element_type.45.row_x, f32[4,3,512]{2,1,0:T(4,128)S(1)} %pad_maximum_fusion.cross_x), custom_call_target="tpu_custom_call" | custom-call | tf_op jit(solution)/shard_map/pallas_call | solution.py:395
  97.8 7.8 %all-to-all-done.4.near = bf16[4,18,64,128]{3,2,1,0:T(8,128)(2,1)S(1)} async-done(((bf16[4,18,64,128]{3,2,1,0:T(8,128)(2,1)}), bf16[4,18,64,128]{3,2,1,0:T(8,128)(2,1)S(1)}, u32[]{:S(2)}, u32[]{:S(2)}) %all-to-all-start.4) | async-done | bytes 1179680 | tf_op jit(solution)/shard_map/all_to_all | solution.py:548
  105.7 3.6 %shard_map.59 = bf16[8,784,128]{2,1,0:T(8,128)(2,1)} custom-call(s32[2]{0:T(128)S(1)} %pad_add_fusion.5.info, s32[1,128]{1,0:T(1,128)S(1)} %get-tuple-element.198.loads, s32[8,256]{1,0:T(8,128)S(1)} %get-tuple-element.199.lists, bf16[4,18,64,128]{3,2,1,0:T(8,128)(2,1)S(1)} %all-to-all-done.4.near), custom_call_target="tpu_custom_call" | custom-call | tf_op jit(solution)/shard_map/pallas_call | solution.py:395
  109.3 3.7 %all-to-all-start.5 = ((bf16[8,784,128]{2,1,0:T(8,128)(2,1)}), bf16[8,784,128]{2,1,0:T(8,128)(2,1)S(1)}, u32[]{:S(2)}, u32[]{:S(2)}) async-start(bf16[8,784,128]{2,1,0:T(8,128)(2,1)} %shard_map.59), calls=%async_computation.5 | async-start | bytes 3211264 | tf_op jit(solution)/shard_map/all_to_all | solution.py:565
  113.2 0.7 convert_multiply_fusion.base
  114.1 1.4 shard_map.55
  115.5 0.9 copy-done
  116.4 4.2 %shard_map.57 = (f32[64,896]{1,0:T(8,128)S(1)}, bf16[16,7,64,128]{3,2,1,0:T(8,128)(2,1)S(1)}, s32[96]{0:T(128)S(1)}) custom-call(s32[16,128]{1,0:T(8,128)S(1)} %get-tuple-element.79.lists, s32[16,128]{1,0:T(8,128)S(1)} %get-tuple-element.201.far.lists, bf16[4,18,64,128]{3,2,1,0:T(8,128)(2,1)} %copy-done.2, bf16[8,464,128]{2,1,0:T(8,128)(2,1)} %copy-done.3, ...), custom_call_target="tpu_custom_call" | custom-call | tf_op jit(solution)/shard_map/pallas_call | solution.py:395
  120.6 0.7 copy-done.1
  121.3 30.4 %all-to-all-done.5.far = bf16[8,784,128]{2,1,0:T(8,128)(2,1)S(1)} async-done(((bf16[8,784,128]{2,1,0:T(8,128)(2,1)}), bf16[8,784,128]{2,1,0:T(8,128)(2,1)S(1)}, u32[]{:S(2)}, u32[]{:S(2)}) %all-to-all-start.5) | async-done | bytes 1605664 | tf_op jit(solution)/shard_map/all_to_all | solution.py:565
  151.7 2.5 %shard_map.60 = (f32[64,896]{1,0:T(8,128)}, s32[1]{0:T(128)}) custom-call(s32[16,128]{1,0:T(8,128)S(1)} %get-tuple-element.201.far.lists, s32[96]{0:T(128)S(1)} %get-tuple-element.82.ahead, f32[64,896]{1,0:T(8,128)} %copy-done.1, bf16[8,784,128]{2,1,0:T(8,128)(2,1)S(1)} %all-to-all-done.5.far, bf16[16,7,64,128]{3,2,1,0:T(8,128)(2,1)S(1)} %get-tuple-element.86.rights), custom_call_target="tpu_custom_call" | custom-call | tf_op jit(solution)/shard_map/pallas_call | solution.py:395
  154.2 0.6 while.12
  (101 shorter events, 3.2 us)
Async XLA Ops:
  6.5 12.6 %copy-start.11 = (s32[1,1,36]{2,1,0:T(1,128)S(1)}, s32[1,1,36]{2,1,0:T(1,128)}, u32[]{:S(2)}) copy-start(s32[1,1,36]{2,1,0:T(1,128)} %param.10) | copy-start | bytes 436
  6.5 12.6 %copy-start.10 = (s32[1,1,36]{2,1,0:T(1,128)S(1)}, s32[1,1,36]{2,1,0:T(1,128)}, u32[]{:S(2)}) copy-start(s32[1,1,36]{2,1,0:T(1,128)} %param.11) | copy-start | bytes 436
  6.5 12.6 %copy-start.13 = (s32[1,1,14]{2,1,0:T(1,128)S(1)}, s32[1,1,14]{2,1,0:T(1,128)}, u32[]{:S(2)}) copy-start(s32[1,1,14]{2,1,0:T(1,128)} %param.8) | copy-start | bytes 172
  6.5 12.6 %copy-start.12 = (s32[1,1,14]{2,1,0:T(1,128)S(1)}, s32[1,1,14]{2,1,0:T(1,128)}, u32[]{:S(2)}) copy-start(s32[1,1,14]{2,1,0:T(1,128)} %param.9) | copy-start | bytes 172
  6.5 74.4 %all-gather.3.cloned.1.call-start = ((), (), s32[]{:S(2)}) async-start(), calls=%async_computation.6 | async-start | bytes 4128768 | tf_op jit(solution)/shard_map/all_gather | solution.py:449
  19.9 17.3 %all-to-all-start.2 = ((s32[32,1,128]{2,1,0:T(1,128)}), s32[32,1,128]{2,1,0:T(1,128)S(1)}, u32[]{:S(2)}, u32[]{:S(2)}) async-start(s32[32,1,128]{2,1,0:T(1,128)} %broadcast_in_dim.84), calls=%async_computation.2 | async-start | bytes 32768 | tf_op jit(solution)/shard_map/all_to_all | solution.py:430
  38.5 33.6 %all-to-all-start.3 = ((bf16[8,464,128]{2,1,0:T(8,128)(2,1)}), bf16[8,464,128]{2,1,0:T(8,128)(2,1)S(1)}, u32[]{:S(2)}, u32[]{:S(2)}) async-start(bf16[8,464,128]{2,1,0:T(8,128)(2,1)} %broadcast_in_dim.87), calls=%async_computation.3 | async-start | bytes 1900544 | tf_op jit(solution)/shard_map/all_to_all | solution.py:430
  72.1 14.5 %copy-start.3 = (bf16[8,464,128]{2,1,0:T(8,128)(2,1)}, bf16[8,464,128]{2,1,0:T(8,128)(2,1)S(1)}, u32[]{:S(2)}) copy-start(bf16[8,464,128]{2,1,0:T(8,128)(2,1)S(1)} %all-to-all-done.3.own_tiles) | copy-start | bytes 2850820
  72.1 8.1 %collective-permute-start = (bf16[8,464,128]{2,1,0:T(8,128)(2,1)S(1)}, bf16[8,464,128]{2,1,0:T(8,128)(2,1)S(1)}, u32[]{:S(2)}, u32[]{:S(2)}) collective-permute-start(bf16[8,464,128]{2,1,0:T(8,128)(2,1)S(1)} %all-to-all-done.3.own_tiles), channel_id=1, source_target_pairs={{0,32},{32,0},{64,96},{96,64},{128,160},{160,128},{192,224},{224,1... | collective-permute-start | bytes 2850824 | tf_op jit(solution)/shard_map/ppermute | solution.py:469
  78.1 0.6 copy-start.8
  80.2 6.4 %copy-start.5 = (bf16[8,464,128]{2,1,0:T(8,128)(2,1)}, bf16[8,464,128]{2,1,0:T(8,128)(2,1)S(1)}, u32[]{:S(2)}) copy-start(bf16[8,464,128]{2,1,0:T(8,128)(2,1)S(1)} %collective-permute-done.other_tiles) | copy-start | bytes 2850820
  86.6 19.1 %all-to-all-start.4 = ((bf16[4,18,64,128]{3,2,1,0:T(8,128)(2,1)}), bf16[4,18,64,128]{3,2,1,0:T(8,128)(2,1)S(1)}, u32[]{:S(2)}, u32[]{:S(2)}) async-start(bf16[4,18,64,128]{3,2,1,0:T(8,128)(2,1)} %shard_map.56), calls=%async_computation.4 | async-start | bytes 2359296 | tf_op jit(solution)/shard_map/all_to_all | solution.py:548
  105.6 3.6 %copy-start.2 = (bf16[4,18,64,128]{3,2,1,0:T(8,128)(2,1)}, bf16[4,18,64,128]{3,2,1,0:T(8,128)(2,1)S(1)}, u32[]{:S(2)}) copy-start(bf16[4,18,64,128]{3,2,1,0:T(8,128)(2,1)S(1)} %all-to-all-done.4.near) | copy-start | bytes 3538948
  109.3 3.9 %copy-start.7 = (bf16[1,1,64,896]{3,2,1,0:T(8,128)(2,1)S(1)}, bf16[1,1,64,896]{3,2,1,0:T(8,128)(2,1)}, u32[]{:S(2)}) copy-start(bf16[1,1,64,896]{3,2,1,0:T(8,128)(2,1)} %param.7) | copy-start | bytes 344068
  109.3 4.6 %copy-start.9 = (f32[2,32,40]{2,1,0:T(8,128)S(1)}, f32[2,32,40]{2,1,0:T(8,128)}, u32[]{:S(2)}) copy-start(f32[2,32,40]{2,1,0:T(8,128)} %copy-done.8) | copy-start | bytes 30724
  109.3 42.4 %all-to-all-start.5 = ((bf16[8,784,128]{2,1,0:T(8,128)(2,1)}), bf16[8,784,128]{2,1,0:T(8,128)(2,1)S(1)}, u32[]{:S(2)}, u32[]{:S(2)}) async-start(bf16[8,784,128]{2,1,0:T(8,128)(2,1)} %shard_map.59), calls=%async_computation.5 | async-start | bytes 3211264 | tf_op jit(solution)/shard_map/all_to_all | solution.py:565
  115.5 0.9 copy-start
  120.6 0.7 copy-start.1
Sparse Core Ops, SparseCore 0:
  19.2 57.4 all-gather.2

commit v5 on v4

--- a/solution.py
+++ b/solution.py
@@ -272,7 +272,7 @@
             squares[n] = square
         return carry
 
-    lax.fori_loop(0, squares.shape[0], store, 0, unroll=2)
+    lax.fori_loop(0, squares.shape[0], store, 0, unroll=6)
     copies = [
         pltpu.make_async_copy(squares, out_ref.at[n], sent.at[n]) for n in range(out_ref.shape[0])
     ]

time: 164 us -> 163 us (level)
    all_to_all x1, starting transfers between devices: 3.73 us -> 5.52 us  [exchange(): lax.all_to_all(packed, 'col', split_axis=0, concat_axis=0, axis_index_gro...]
    all_to_all x1, waiting for transfers between devices: 7.85 us -> 6.2 us  [per_device(): lax.all_to_all(square, 'col', split_axis=0, concat_axis=0, axis_index_gro...]
where the time goes in v5:
time: 163 us; the launch traced here: 161 us
  waiting for transfers between devices  68.3 us (42%)
  starting transfers between devices  33.9 us (21%)
  Pallas kernels  22.9 us (14%)
  between operations  13.9 us (9%)
  blocking collectives  11.3 us (7%)
  local copies, waits for them, and re-layouts  8.07 us (5%)
    all_to_all x2, waiting for transfers between devices, send_all(): return lax.all_to_all(copies, axis, split_axis=0, concat_axis=0, **groups)  30.8 us
    all_to_all x1, waiting for transfers between devices, exchange(): lax.all_to_all(packed, 'col', split_axis=0, concat_axis=0, axis_index_gro...  30.6 us
    pallas_call x6, Pallas kernels, call(): pl.pallas_call(kernel, out_shape=out, in_specs=[SMEM] * len(scalars) + [p...  22.9 us
    all_to_all x2, starting transfers between devices, send_all(): return lax.all_to_all(copies, axis, split_axis=0, concat_axis=0, **groups)  18.8 us
    all_to_all x1, blocking collectives, send_all(): return lax.all_to_all(copies, axis, split_axis=0, concat_axis=0, **groups)  11.3 us
    all_to_all x1, waiting for transfers between devices, per_device(): lax.all_to_all(square, 'col', split_axis=0, concat_axis=0, axis_index_gro...  6.2 us
    ppermute x1, starting transfers between devices, per_device(): lax.ppermute(own_tiles, 'row', [(n, n ^ 1) for n in range(n_row)])  5.94 us
    all_to_all x1, starting transfers between devices, exchange(): lax.all_to_all(packed, 'col', split_axis=0, concat_axis=0, axis_index_gro...  5.52 us
  transfers between devices with their start and end apart: 6, of which 5 were waited for; matrix products, arithmetic and copies ran while one was open for 4% of the time, Pallas kernels for 7%

profile of v5, /device:TPU:1, one launch (start us, length us, event | category | flops | bytes accessed | tf_op | source)
XLA Modules:
  0.0 160.6 jit_solution(1786849345054739389)
XLA Ops:
  6.6 1.1 reshape_squeeze.3
  7.7 11.3 %all_to_all.31 = bf16[4,448,128]{2,1,0:T(8,128)(2,1)} all-to-all(bf16[4,448,128]{2,1,0:T(8,128)(2,1)S(1)} %broadcast_in_dim.83), channel_id=1, replica_groups={{0,1,2,3},{4,5,6,7},{8,9,10,11},{12,13,14,15},{16,17,18,19},{20,21,22,2..., dimensions={0} | all-to-all | bytes 917504 | tf_op jit(solution)/shard_map/all_to_all | solution.py:430
  19.3 0.6 broadcast_in_dim.84
  19.9 8.8 %all-to-all-start.2 = ((s32[32,1,128]{2,1,0:T(1,128)}), s32[32,1,128]{2,1,0:T(1,128)S(1)}, u32[]{:S(2)}, u32[]{:S(2)}) async-start(s32[32,1,128]{2,1,0:T(1,128)} %broadcast_in_dim.84), calls=%async_computation.2 | async-start | bytes 32768 | tf_op jit(solution)/shard_map/all_to_all | solution.py:430
  28.8 8.4 %all-to-all-done.2 = s32[32,1,128]{2,1,0:T(1,128)S(1)} async-done(((s32[32,1,128]{2,1,0:T(1,128)}), s32[32,1,128]{2,1,0:T(1,128)S(1)}, u32[]{:S(2)}, u32[]{:S(2)}) %all-to-all-start.2) | async-done | bytes 16416 | tf_op jit(solution)/shard_map/all_to_all | solution.py:430
  37.4 1.1 broadcast_in_dim.87
  38.5 10.0 %all-to-all-start.3 = ((bf16[8,464,128]{2,1,0:T(8,128)(2,1)}), bf16[8,464,128]{2,1,0:T(8,128)(2,1)S(1)}, u32[]{:S(2)}, u32[]{:S(2)}) async-start(bf16[8,464,128]{2,1,0:T(8,128)(2,1)} %broadcast_in_dim.87), calls=%async_computation.3 | async-start | bytes 1900544 | tf_op jit(solution)/shard_map/all_to_all | solution.py:430
  49.7 22.3 %all-to-all-done.3.own_tiles = bf16[8,464,128]{2,1,0:T(8,128)(2,1)S(1)} async-done(((bf16[8,464,128]{2,1,0:T(8,128)(2,1)}), bf16[8,464,128]{2,1,0:T(8,128)(2,1)S(1)}, u32[]{:S(2)}, u32[]{:S(2)}) %all-to-all-start.3) | async-done | bytes 950304 | tf_op jit(solution)/shard_map/all_to_all | solution.py:430
  72.1 5.9 %collective-permute-start = (bf16[8,464,128]{2,1,0:T(8,128)(2,1)S(1)}, bf16[8,464,128]{2,1,0:T(8,128)(2,1)S(1)}, u32[]{:S(2)}, u32[]{:S(2)}) collective-permute-start(bf16[8,464,128]{2,1,0:T(8,128)(2,1)S(1)} %all-to-all-done.3.own_tiles), channel_id=1, source_target_pairs={{0,32},{32,0},{64,96},{96,64},{128,160},{160,128},{192,224},{224,1... | collective-permute-start | bytes 2850824 | tf_op jit(solution)/shard_map/ppermute | solution.py:469
  78.1 0.6 copy-done.8
  78.8 0.1 reshape.546
  78.9 0.1 copy.47
  79.4 0.7 collective-permute-done.other_tiles
  80.2 0.1 reshape.548
  80.3 0.1 copy.48
  80.9 5.2 %shard_map.56 = bf16[4,18,64,128]{3,2,1,0:T(8,128)(2,1)} custom-call(bf16[32,448,128]{2,1,0:T(8,128)(2,1)} %all-gather.3.cloned.1.call-done.row_hbm, f32[2,128]{1,0:T(2,128)S(1)} %pad_convert_fusion.own_z, f32[2,512]{1,0:T(2,128)S(1)} %convert_element_type.45.row_x, f32[2,128]{1,0:T(2,128)S(1)} %maximum_select_fusion.1.own_col, ...), custom_call_target="tpu_custom_call" | custom-call | tf_op jit(solution)/shard_map/pallas_call | solution.py:395
  86.2 3.5 %all-to-all-start.4 = ((bf16[4,18,64,128]{3,2,1,0:T(8,128)(2,1)}), bf16[4,18,64,128]{3,2,1,0:T(8,128)(2,1)S(1)}, u32[]{:S(2)}, u32[]{:S(2)}) async-start(bf16[4,18,64,128]{3,2,1,0:T(8,128)(2,1)} %shard_map.56), calls=%async_computation.4 | async-start | bytes 2359296 | tf_op jit(solution)/shard_map/all_to_all | solution.py:548
  89.8 0.1 squeeze.11
  90.0 0.1 stack.78
  90.2 0.1 broadcast_in_dim.93.near_z
  90.3 6.4 %shard_map.58 = (s32[8,256]{1,0:T(8,128)S(1)}, s32[1,128]{1,0:T(1,128)S(1)}) custom-call(f32[2,160,128]{2,1,0:T(8,128)S(1)} %broadcast_in_dim.93.near_z, f32[2,512]{1,0:T(2,128)S(1)} %convert_element_type.45.row_x, f32[4,3,512]{2,1,0:T(4,128)S(1)} %pad_maximum_fusion.cross_x), custom_call_target="tpu_custom_call" | custom-call | tf_op jit(solution)/shard_map/pallas_call | solution.py:395
  96.7 6.2 %all-to-all-done.4.near = bf16[4,18,64,128]{3,2,1,0:T(8,128)(2,1)S(1)} async-done(((bf16[4,18,64,128]{3,2,1,0:T(8,128)(2,1)}), bf16[4,18,64,128]{3,2,1,0:T(8,128)(2,1)S(1)}, u32[]{:S(2)}, u32[]{:S(2)}) %all-to-all-start.4) | async-done | bytes 1179680 | tf_op jit(solution)/shard_map/all_to_all | solution.py:548
  103.0 3.2 %shard_map.59 = bf16[8,784,128]{2,1,0:T(8,128)(2,1)} custom-call(s32[2]{0:T(128)S(1)} %pad_add_fusion.5.info, s32[1,128]{1,0:T(1,128)S(1)} %get-tuple-element.198.loads, s32[8,256]{1,0:T(8,128)S(1)} %get-tuple-element.199.lists, bf16[4,18,64,128]{3,2,1,0:T(8,128)(2,1)S(1)} %all-to-all-done.4.near), custom_call_target="tpu_custom_call" | custom-call | tf_op jit(solution)/shard_map/pallas_call | solution.py:395
  106.2 5.5 %all-to-all-start.5 = ((bf16[8,784,128]{2,1,0:T(8,128)(2,1)}), bf16[8,784,128]{2,1,0:T(8,128)(2,1)S(1)}, u32[]{:S(2)}, u32[]{:S(2)}) async-start(bf16[8,784,128]{2,1,0:T(8,128)(2,1)} %shard_map.59), calls=%async_computation.5 | async-start | bytes 3211264 | tf_op jit(solution)/shard_map/all_to_all | solution.py:565
  111.8 0.7 convert_multiply_fusion.base
  112.7 1.4 shard_map.55
  114.1 0.9 copy-done
  115.1 4.2 %shard_map.57 = (f32[64,896]{1,0:T(8,128)S(1)}, bf16[16,7,64,128]{3,2,1,0:T(8,128)(2,1)S(1)}, s32[96]{0:T(128)S(1)}) custom-call(s32[16,128]{1,0:T(8,128)S(1)} %get-tuple-element.79.lists, s32[16,128]{1,0:T(8,128)S(1)} %get-tuple-element.201.far.lists, bf16[4,18,64,128]{3,2,1,0:T(8,128)(2,1)} %copy-done.2, bf16[8,464,128]{2,1,0:T(8,128)(2,1)} %copy-done.3, ...), custom_call_target="tpu_custom_call" | custom-call | tf_op jit(solution)/shard_map/pallas_call | solution.py:395
  119.3 0.7 copy-done.1
  120.0 30.6 %all-to-all-done.5.far = bf16[8,784,128]{2,1,0:T(8,128)(2,1)S(1)} async-done(((bf16[8,784,128]{2,1,0:T(8,128)(2,1)}), bf16[8,784,128]{2,1,0:T(8,128)(2,1)S(1)}, u32[]{:S(2)}, u32[]{:S(2)}) %all-to-all-start.5) | async-done | bytes 1605664 | tf_op jit(solution)/shard_map/all_to_all | solution.py:565
  150.6 2.5 %shard_map.60 = (f32[64,896]{1,0:T(8,128)}, s32[1]{0:T(128)}) custom-call(s32[16,128]{1,0:T(8,128)S(1)} %get-tuple-element.201.far.lists, s32[96]{0:T(128)S(1)} %get-tuple-element.82.ahead, f32[64,896]{1,0:T(8,128)} %copy-done.1, bf16[8,784,128]{2,1,0:T(8,128)(2,1)S(1)} %all-to-all-done.5.far, bf16[16,7,64,128]{3,2,1,0:T(8,128)(2,1)S(1)} %get-tuple-element.86.rights), custom_call_target="tpu_custom_call" | custom-call | tf_op jit(solution)/shard_map/pallas_call | solution.py:395
  153.1 0.6 while.12
  (101 shorter events, 3.2 us)
Async XLA Ops:
  6.5 12.6 %copy-start.11 = (s32[1,1,36]{2,1,0:T(1,128)S(1)}, s32[1,1,36]{2,1,0:T(1,128)}, u32[]{:S(2)}) copy-start(s32[1,1,36]{2,1,0:T(1,128)} %param.10) | copy-start | bytes 436
  6.5 12.6 %copy-start.10 = (s32[1,1,36]{2,1,0:T(1,128)S(1)}, s32[1,1,36]{2,1,0:T(1,128)}, u32[]{:S(2)}) copy-start(s32[1,1,36]{2,1,0:T(1,128)} %param.11) | copy-start | bytes 436
  6.5 12.6 %copy-start.13 = (s32[1,1,14]{2,1,0:T(1,128)S(1)}, s32[1,1,14]{2,1,0:T(1,128)}, u32[]{:S(2)}) copy-start(s32[1,1,14]{2,1,0:T(1,128)} %param.8) | copy-start | bytes 172
  6.5 12.6 %copy-start.12 = (s32[1,1,14]{2,1,0:T(1,128)S(1)}, s32[1,1,14]{2,1,0:T(1,128)}, u32[]{:S(2)}) copy-start(s32[1,1,14]{2,1,0:T(1,128)} %param.9) | copy-start | bytes 172
  6.5 74.4 %all-gather.3.cloned.1.call-start = ((), (), s32[]{:S(2)}) async-start(), calls=%async_computation.6 | async-start | bytes 4128768 | tf_op jit(solution)/shard_map/all_gather | solution.py:449
  19.9 17.3 %all-to-all-start.2 = ((s32[32,1,128]{2,1,0:T(1,128)}), s32[32,1,128]{2,1,0:T(1,128)S(1)}, u32[]{:S(2)}, u32[]{:S(2)}) async-start(s32[32,1,128]{2,1,0:T(1,128)} %broadcast_in_dim.84), calls=%async_computation.2 | async-start | bytes 32768 | tf_op jit(solution)/shard_map/all_to_all | solution.py:430
  38.5 33.6 %all-to-all-start.3 = ((bf16[8,464,128]{2,1,0:T(8,128)(2,1)}), bf16[8,464,128]{2,1,0:T(8,128)(2,1)S(1)}, u32[]{:S(2)}, u32[]{:S(2)}) async-start(bf16[8,464,128]{2,1,0:T(8,128)(2,1)} %broadcast_in_dim.87), calls=%async_computation.3 | async-start | bytes 1900544 | tf_op jit(solution)/shard_map/all_to_all | solution.py:430
  72.1 14.1 %copy-start.3 = (bf16[8,464,128]{2,1,0:T(8,128)(2,1)}, bf16[8,464,128]{2,1,0:T(8,128)(2,1)S(1)}, u32[]{:S(2)}) copy-start(bf16[8,464,128]{2,1,0:T(8,128)(2,1)S(1)} %all-to-all-done.3.own_tiles) | copy-start | bytes 2850820
  72.1 8.1 %collective-permute-start = (bf16[8,464,128]{2,1,0:T(8,128)(2,1)S(1)}, bf16[8,464,128]{2,1,0:T(8,128)(2,1)S(1)}, u32[]{:S(2)}, u32[]{:S(2)}) collective-permute-start(bf16[8,464,128]{2,1,0:T(8,128)(2,1)S(1)} %all-to-all-done.3.own_tiles), channel_id=1, source_target_pairs={{0,32},{32,0},{64,96},{96,64},{128,160},{160,128},{192,224},{224,1... | collective-permute-start | bytes 2850824 | tf_op jit(solution)/shard_map/ppermute | solution.py:469
  78.1 0.6 copy-start.8
  80.2 6.0 %copy-start.5 = (bf16[8,464,128]{2,1,0:T(8,128)(2,1)}, bf16[8,464,128]{2,1,0:T(8,128)(2,1)S(1)}, u32[]{:S(2)}) copy-start(bf16[8,464,128]{2,1,0:T(8,128)(2,1)S(1)} %collective-permute-done.other_tiles) | copy-start | bytes 2850820
  86.2 16.8 %all-to-all-start.4 = ((bf16[4,18,64,128]{3,2,1,0:T(8,128)(2,1)}), bf16[4,18,64,128]{3,2,1,0:T(8,128)(2,1)S(1)}, u32[]{:S(2)}, u32[]{:S(2)}) async-start(bf16[4,18,64,128]{3,2,1,0:T(8,128)(2,1)} %shard_map.56), calls=%async_computation.4 | async-start | bytes 2359296 | tf_op jit(solution)/shard_map/all_to_all | solution.py:548
  102.9 3.2 %copy-start.2 = (bf16[4,18,64,128]{3,2,1,0:T(8,128)(2,1)}, bf16[4,18,64,128]{3,2,1,0:T(8,128)(2,1)S(1)}, u32[]{:S(2)}) copy-start(bf16[4,18,64,128]{3,2,1,0:T(8,128)(2,1)S(1)} %all-to-all-done.4.near) | copy-start | bytes 3538948
  106.1 5.7 %copy-start.7 = (bf16[1,1,64,896]{3,2,1,0:T(8,128)(2,1)S(1)}, bf16[1,1,64,896]{3,2,1,0:T(8,128)(2,1)}, u32[]{:S(2)}) copy-start(bf16[1,1,64,896]{3,2,1,0:T(8,128)(2,1)} %param.7) | copy-start | bytes 344068
  106.1 6.4 %copy-start.9 = (f32[2,32,40]{2,1,0:T(8,128)S(1)}, f32[2,32,40]{2,1,0:T(8,128)}, u32[]{:S(2)}) copy-start(f32[2,32,40]{2,1,0:T(8,128)} %copy-done.8) | copy-start | bytes 30724
  106.2 44.4 %all-to-all-start.5 = ((bf16[8,784,128]{2,1,0:T(8,128)(2,1)}), bf16[8,784,128]{2,1,0:T(8,128)(2,1)S(1)}, u32[]{:S(2)}, u32[]{:S(2)}) async-start(bf16[8,784,128]{2,1,0:T(8,128)(2,1)} %shard_map.59), calls=%async_computation.5 | async-start | bytes 3211264 | tf_op jit(solution)/shard_map/all_to_all | solution.py:565
  114.1 0.9 copy-start
  119.3 0.7 copy-start.1
Sparse Core Ops, SparseCore 0:
  19.2 57.4 all-gather.2
